TPU v7x, 128 devices: a whole 4x4x4 slice. The times are simulated.
128 devices in a mesh: gore: 16 (over y, z_lo, core), band: 8 (over x, z_hi).
Axes of the slice: x: 4, y: 4, z: 4 (z_hi: 2, z_lo: 2; z = z_hi * 2 + z_lo), core: 2. Of those that a mesh axis runs over, the one named last changes fastest.
Arguments:
- displacement: float32 [3, 2048, 2048], P(None, 'gore', 'band'), may hold values from -2.5 to 2.5
- stiffness: float32 [2048, 2048], P('gore', 'band'), may hold values from 0.5 to 4
- pressure: float32 [2048, 2048], P('gore', 'band'), may hold values from 0.5 to 1.5
- yield_points: int32 [1024], P(('gore', 'band')), may hold values from 0 to 32767, as said below
- route: int32 [1024, 1], P(('gore', 'band')), may hold values from 0 to 15; in each aligned block of 8 rows (0 to 7, 8 to 15, ...) at most 2 rows name the same one
- cell_state: float32 [1024, 3, 13824], P(('gore', 'band')), may hold values from -3 to 3
- weave: float32 [13824], replicated, may hold values from 1 to 8
Outputs:
- nodal_force: float32 [3, 2048, 2048], P(None, 'gore', 'band')
- cell_strain: float32 [4096, 3, 13824], P(('gore', 'band'))
Inputs may be any that keep to these rules, and one draw needn't show every extreme that they name: `yield_points`: the 8 entries of one device are distinct node numbers of its 128 x 256 block, counted row by row. `route`: among the 8 rows of one device no worker index appears more than 2 times, and some device reaches 2.
All inputs are finite; a program needn't handle non-finite values.
Results may differ from a plain program's by a relative error of at most 0.0001.
Values sent between devices are 32-bit elements; how exact they have to be, the bound alone decides.
A program may use at most 192 MiB of HBM per device.

v0:
```python
import math

import jax
import jax.numpy as jnp
from jax import lax
from jax.sharding import PartitionSpec as P

G = 24
SWEEPS = 2


BETA = 0.5
REFERENCE_STIFF = 10.0
POISSON = 0.3
HIGHEST = lax.Precision.HIGHEST


def padded_2(cells, sides, width):
    for axis, dim in sides:
        count = lax.axis_size(axis)
        head = lax.slice_in_dim(cells, 0, width, axis=dim)
        tail = lax.slice_in_dim(cells, cells.shape[dim] - width, cells.shape[dim], axis=dim)
        cells = jnp.concatenate(
            [
                lax.ppermute(tail, axis, [(i, (i + 1) % count) for i in range(count)]),
                cells,
                lax.ppermute(head, axis, [((i + 1) % count, i) for i in range(count)]),
            ],
            axis=dim,
        )
    return cells


def spectral_weight(grid_side):
    wave_index = jnp.arange(grid_side, dtype=jnp.int32)
    sines = jnp.sin(wave_index.astype(jnp.float32) * (2.0 * math.pi / grid_side))
    square = sines * sines
    summed = square[:, None, None] + square[None, :, None] + square[None, None, :]
    level = wave_index % (grid_side // 2) == 0
    silent = level[:, None, None] & level[None, :, None] & level[None, None, :]
    return jnp.where(silent, 0.0, 1.0 / (REFERENCE_STIFF * jnp.where(silent, 1.0, summed)))


def line_tables(grid_side):
    wave_index = jnp.arange(grid_side, dtype=jnp.int32)
    product = wave_index[:, None] * wave_index[None, :] % grid_side
    angles = product.astype(jnp.float32) * (2.0 * math.pi / grid_side)
    return (jnp.cos(angles), jnp.sin(angles))


def plane_tables(grid_side):
    plane = grid_side * grid_side
    index = jnp.arange(plane, dtype=jnp.int32)
    upper_part = index // grid_side
    lower_part = index % grid_side
    phase = (
        upper_part[:, None] * upper_part[None, :] + lower_part[:, None] * lower_part[None, :]
    ) % grid_side
    angles = phase.astype(jnp.float32) * (2.0 * math.pi / grid_side)
    return (jnp.cos(angles), jnp.sin(angles))


def plane_product(values, table):
    return jnp.einsum("nxp,pq->nxq", values, table, precision=HIGHEST)


def line_product(table, values):
    return jnp.einsum("kx,nxq->nkq", table, values, precision=HIGHEST)


def along_line(values):
    return (jnp.roll(values, -1, -2) - jnp.roll(values, 1, -2)) * 0.5


def along_upper(values):
    return (jnp.roll(values, -G, -1) - jnp.roll(values, G, -1)) * 0.5


def along_lower(values, lower_index):
    forward_value = jnp.where(
        lower_index == G - 1, jnp.roll(values, G - 1, -1), jnp.roll(values, -1, -1)
    )
    backward_value = jnp.where(
        lower_index == 0, jnp.roll(values, 1 - G, -1), jnp.roll(values, 1, -1)
    )
    return (forward_value - backward_value) * 0.5


def yarn_law(strain_field, stiff_field):
    magnitude = jnp.sum(strain_field * strain_field, axis=1, keepdims=True)
    return stiff_field * (1.0 + BETA * magnitude / (1.0 + magnitude)) * strain_field


def solve_cells(states, drives, weave):
    cell_count = states.shape[0]
    plane = G * G
    strain_field = states.reshape(cell_count, 3, G, plane)
    strain_field = (
        strain_field - jnp.mean(strain_field, axis=(2, 3), keepdims=True) + drives[:, :, None, None]
    )
    stiff_field = weave.reshape(G, plane)
    cos_line, sin_line = line_tables(G)
    cos_plane, sin_plane = plane_tables(G)
    weight = spectral_weight(G).reshape(G, plane)
    lower_index = jnp.arange(plane, dtype=jnp.int32) % G
    inverse_scale = 1.0 / (G * G * G)
    for iteration in range(SWEEPS):
        stress_field = yarn_law(strain_field, stiff_field)
        source = (
            along_line(stress_field[:, 0])
            + along_upper(stress_field[:, 1])
            + along_lower(stress_field[:, 2], lower_index)
        )
        real_part = plane_product(source, cos_plane)
        imag_part = -plane_product(source, sin_plane)
        spec_real = (line_product(cos_line, real_part) + line_product(sin_line, imag_part)) * weight
        spec_imag = (line_product(cos_line, imag_part) - line_product(sin_line, real_part)) * weight
        back_real = line_product(cos_line, spec_real) - line_product(sin_line, spec_imag)
        back_imag = line_product(cos_line, spec_imag) + line_product(sin_line, spec_real)
        potential = (
            plane_product(back_real, cos_plane) - plane_product(back_imag, sin_plane)
        ) * inverse_scale
        strain_field = strain_field + jnp.stack(
            [along_line(potential), along_upper(potential), along_lower(potential, lower_index)],
            axis=1,
        )
    stress_field = yarn_law(strain_field, stiff_field)
    new_states = strain_field.reshape(cell_count, 3, G * G * G)
    return (new_states, jnp.mean(stress_field, axis=(2, 3)))


def close_band(padded, band_place, total_bands):
    column = jnp.arange(padded.shape[2], dtype=jnp.int32)
    outside = (column == 0) & (band_place == 0) | (column == padded.shape[2] - 1) & (
        band_place == total_bands - 1
    )
    return jnp.where(outside[None, None, :], 0.0, padded)


def along_gore(padded):
    return (padded[:, 2:, 1:-1] - padded[:, :-2, 1:-1]) * 0.5


def along_band(padded):
    return (padded[:, 1:-1, 2:] - padded[:, 1:-1, :-2]) * 0.5


def local(displacement, stiffness, pressure, yield_points, route, cell_state, weave):
    gore_count = lax.axis_size("gore")
    band_count = lax.axis_size("band")
    band_place = lax.axis_index("band")
    cap_count = yield_points.shape[0]
    most_count = max(2, (cap_count + gore_count - 1) // gore_count)
    slot_count = gore_count * most_count
    voxels = cell_state.shape[2]
    padded = padded_2(displacement, (("gore", 1), ("band", 2)), 1)
    padded = close_band(padded, band_place, band_count)
    gore_slope = along_gore(padded)
    band_slope = along_band(padded)
    strain = jnp.stack(
        [
            gore_slope[0] + 0.5 * gore_slope[2] * gore_slope[2],
            band_slope[1] + 0.5 * band_slope[2] * band_slope[2],
            0.5 * (band_slope[0] + gore_slope[1]) + 0.5 * gore_slope[2] * band_slope[2],
        ]
    )
    cell_drive = jnp.take(strain.reshape(3, -1), yield_points, axis=1).T
    workers = route[:, 0]
    onehot = (workers[:, None] == jnp.arange(gore_count, dtype=jnp.int32)[None, :]).astype(
        jnp.int32
    )
    earlier = jnp.cumsum(onehot, axis=0) - onehot
    slot_index = workers * most_count + jnp.sum(earlier * onehot, axis=1)
    own_states, point_stress = solve_cells(cell_state, cell_drive, weave)
    outgoing = jnp.zeros((slot_count, 3, voxels), jnp.float32).at[slot_index].set(own_states)
    arrived = lax.all_to_all(
        outgoing.reshape(gore_count, most_count, 3, voxels),
        "gore",
        split_axis=0,
        concat_axis=0,
        tiled=True,
    )
    cell_strain = arrived.reshape(slot_count, 3, voxels)
    stress = jnp.stack(
        [
            stiffness * (strain[0] + POISSON * strain[1]),
            stiffness * (strain[1] + POISSON * strain[0]),
            stiffness * (1.0 - POISSON) * strain[2],
        ]
    )
    node_shape = stress.shape
    stress = stress.reshape(3, -1).at[:, yield_points].set(point_stress.T).reshape(node_shape)
    fluxes = jnp.stack(
        [
            stress[0],
            stress[2],
            stress[1],
            stress[0] * gore_slope[2] + stress[2] * band_slope[2],
            stress[2] * gore_slope[2] + stress[1] * band_slope[2],
        ]
    )
    flux_rim = padded_2(fluxes, (("gore", 1), ("band", 2)), 1)
    flux_rim = close_band(flux_rim, band_place, band_count)
    gore_flux = along_gore(flux_rim)
    band_flux = along_band(flux_rim)
    nodal_force = jnp.stack(
        [
            gore_flux[0] + band_flux[1],
            gore_flux[1] + band_flux[2],
            gore_flux[3] + band_flux[4] + pressure,
        ]
    )
    return (nodal_force, cell_strain)


def solution(mesh):
    return jax.shard_map(
        local,
        mesh=mesh,
        in_specs=(
            P(None, "gore", "band"),
            P("gore", "band"),
            P("gore", "band"),
            P(("gore", "band")),
            P(("gore", "band"), None),
            P(("gore", "band"), None, None),
            P(),
        ),
        out_specs=(P(None, "gore", "band"), P(("gore", "band"), None, None)),
        check_vma=False,
    )
```

profile of v0, /device:TPU:24, one launch (start us, length us, event | category | flops | bytes accessed | tf_op | source)
XLA Modules:
  0.0 313.4 jit_solution(13872520383379119040)
XLA Ops:
  1.5 1.5 collective-permute-start.1
  4.4 1.5 reduce_sum.56
  8.8 5.8 %collective-permute-start.3 = (f32[3,130,1]{2,1,0:T(8,128)}, f32[3,130,1]{2,1,0:T(8,128)}, u32[]{:S(2)}, u32[]{:S(2)}) collective-permute-start(f32[3,130,1]{2,1,0:T(8,128)} %get-tuple-element.96), channel_id=1, source_target_pairs={{1,0},{2,1},{3,2},{4,3},{5,4},{6,5},{7,6},{0,7},{9,8},{10,9},{11,1... | collective-permute-start | bytes 4688 | tf_op jit(solution)/shard_map/ppermute | solution.py:27
  15.4 4.7 %collective-permute-done.3 = f32[3,130,1]{2,1,0:T(8,128)} collective-permute-done((f32[3,130,1]{2,1,0:T(8,128)}, f32[3,130,1]{2,1,0:T(8,128)}, u32[]{:S(2)}, u32[]{:S(2)}) %collective-permute-start.3) | collective-permute-done | bytes 1592 | tf_op jit(solution)/shard_map/ppermute | solution.py:27
  20.1 5.8 %collective-permute-done.2 = f32[3,130,1]{2,1,0:T(8,128)} collective-permute-done((f32[3,130,1]{2,1,0:T(8,128)}, f32[3,130,1]{2,1,0:T(8,128)}, u32[]{:S(2)}, u32[]{:S(2)}) %collective-permute-start.2) | collective-permute-done | bytes 1592 | tf_op jit(solution)/shard_map/ppermute | solution.py:25
  25.9 1.3 maximum_select_fusion.1
  30.0 9.2 %copy.56 = f32[3,32768]{0,1:T(8,128)} copy(f32[3,32768]{1,0:T(4,128)} %pad_maximum_fusion.2) | data formatting | bytes 786432 | tf_op jit(solution)/shard_map/stack | solution.py:160
  39.2 6.3 %gather_fusion = f32[8,3]{1,0:T(8,128)S(1)} fusion(f32[3,32768]{0,1:T(8,128)} %copy.56, s32[1024]{0:T(1024)S(1)} %pad_clamp_fusion), kind=kCustom, calls=%fused_computation | custom fusion | bytes 224 | tf_op jit(solution)/shard_map/jit(_take)/gather | solution.py:167
  46.8 1.9 add.452
  51.7 7.3 %fusion.23 = f32[8,24,576]{2,1,0:T(8,128)S(1)} fusion(f32[8,24,576]{2,1,0:T(8,128)S(1)} %fusion.67, s32[576]{0:T(1024)S(1)} %get-tuple-element.105, s32[576]{0:T(1024)S(1)} %get-tuple-element.104), kind=kOutput, calls=%fused_computation.40 | convolution fusion | flops 768172032 | bytes 889344 | tf_op jit(solution)/shard_map/nxp,pq->nxq/dot_general | solution.py:64
  59.1 7.6 %fusion.17 = f32[8,24,576]{2,1,0:T(8,128)S(1)} fusion(f32[8,24,576]{2,1,0:T(8,128)S(1)} %fusion.67, s32[576]{0:T(1024)S(1)} %get-tuple-element.105, s32[576]{0:T(1024)S(1)} %get-tuple-element.104), kind=kOutput, calls=%fused_computation.25 | convolution fusion | flops 768061440 | bytes 889344 | tf_op jit(solution)/shard_map/nxp,pq->nxq/dot_general | solution.py:64
  70.9 7.5 %fusion.7 = f32[8,24,576]{2,1,0:T(8,128)S(1)} fusion(f32[8,24,576]{2,1,0:T(8,128)S(1)} %fusion.47, s32[576]{0:T(1024)S(1)} %get-tuple-element.105, s32[576]{0:T(1024)S(1)} %get-tuple-element.104), kind=kOutput, calls=%fused_computation.15 | convolution fusion | flops 768061440 | bytes 889344 | tf_op jit(solution)/shard_map/nxp,pq->nxq/dot_general | solution.py:64
  79.0 7.5 %fusion.38 = f32[8,24,576]{2,1,0:T(8,128)S(1)} fusion(f32[8,24,576]{2,1,0:T(8,128)S(1)} %fusion.7, f32[8,24,576]{2,1,0:T(8,128)S(1)} %fusion.48, s32[576]{0:T(1024)S(1)} %get-tuple-element.105, s32[576]{0:T(1024)S(1)} %get-tuple-element.104), kind=kOutput, calls=%fused_computation.45 | convolution fusion | flops 768282624 | bytes 1331712 | tf_op jit(solution)/shard_map/nxp,pq->nxq/dot_general | solution.py:64
  90.0 1.8 subtract_multiply_fusion
  91.8 2.0 concatenate.318
  93.8 2.0 concatenate.322
  95.7 2.0 concatenate.310
  97.7 1.9 concatenate.314
  99.7 2.2 fusion.70
  101.9 1.9 mul.718
  103.8 2.1 fusion.69
  105.9 2.0 mul.716
  107.8 1.6 subtract_multiply_fusion.2
  111.2 2.0 add.477
  114.2 1.7 fusion.2
  118.0 7.7 %fusion.26 = f32[8,24,576]{2,1,0:T(8,128)S(1)} fusion(f32[8,24,576]{2,1,0:T(8,128)S(1)} %fusion.73, s32[576]{0:T(1024)S(1)} %copy-done.37, s32[576]{0:T(1024)S(1)} %copy-done.35), kind=kOutput, calls=%fused_computation.41 | convolution fusion | flops 768172032 | bytes 889344 | tf_op jit(solution)/shard_map/nxp,pq->nxq/dot_general | solution.py:64
  125.7 7.2 %fusion.13 = f32[8,24,576]{2,1,0:T(8,128)S(1)} fusion(f32[8,24,576]{2,1,0:T(8,128)S(1)} %fusion.73, s32[576]{0:T(1024)S(1)} %copy-done.37, s32[576]{0:T(1024)S(1)} %copy-done.35), kind=kOutput, calls=%fused_computation.21 | convolution fusion | flops 768061440 | bytes 889344 | tf_op jit(solution)/shard_map/nxp,pq->nxq/dot_general | solution.py:64
  137.3 7.3 %fusion.3 = f32[8,24,576]{2,1,0:T(8,128)S(1)} fusion(f32[8,24,576]{2,1,0:T(8,128)S(1)} %fusion.41, s32[576]{0:T(1024)S(1)} %copy-done.37, s32[576]{0:T(1024)S(1)} %copy-done.35), kind=kOutput, calls=%fused_computation.11 | convolution fusion | flops 768061440 | bytes 889344 | tf_op jit(solution)/shard_map/nxp,pq->nxq/dot_general | solution.py:64
  145.2 7.5 %fusion.35 = f32[8,24,576]{2,1,0:T(8,128)S(1)} fusion(f32[8,24,576]{2,1,0:T(8,128)S(1)} %fusion.3, f32[8,24,576]{2,1,0:T(8,128)S(1)} %fusion.42, s32[576]{0:T(1024)S(1)} %copy-done.37, s32[576]{0:T(1024)S(1)} %copy-done.35), kind=kOutput, calls=%fused_computation.44 | convolution fusion | flops 768282624 | bytes 1331712 | tf_op jit(solution)/shard_map/nxp,pq->nxq/dot_general | solution.py:64
  161.1 1.2 pad_maximum_fusion.10
  163.3 1.2 pad_maximum_fusion.7
  167.5 1.5 fusion.76
  171.8 1.7 subtract_multiply_fusion.1
  175.1 2.1 copy.65
  177.2 3.7 %broadcast_in_dim.124 = f32[32,3,13824]{2,1,0:T(4,128)} broadcast(f32[]{:T(128)} %constant.48.clone.1), dimensions={} | broadcast | bytes 5308420 | tf_op jit(solution)/shard_map/broadcast_in_dim | solution.py:175
  180.9 5.7 %scatter_fusion.1 = f32[32,3,13824]{2,1,0:T(4,128)} fusion(f32[32,3,13824]{2,1,0:T(4,128)} %broadcast_in_dim.124, s32[8]{0:T(128)S(1)} %copy-done.43, f32[8,3,13824]{2,1,0:T(4,128)} %copy.65), kind=kCustom, calls=%fused_computation.2 | custom fusion | bytes 3981344 | tf_op jit(solution)/shard_map/scatter | solution.py:175
  186.6 8.1 %copy.66 = f32[16,2,3,13824]{3,1,2,0:T(2,128)} copy(f32[16,2,3,13824]{3,2,1,0:T(4,128)} %bitcast.305) | data formatting | bytes 10616832 | tf_op jit(solution)/shard_map/reshape | solution.py:177
  194.7 5.9 %all-to-all-start = ((f32[16,2,3,13824]{3,1,2,0:T(2,128)}), f32[16,2,3,13824]{3,1,2,0:T(2,128)}, u32[]{:S(2)}, u32[]{:S(2)}) async-start(f32[16,2,3,13824]{3,1,2,0:T(2,128)} %copy.66), calls=%async_computation | async-start | bytes 10616832 | tf_op jit(solution)/shard_map/all_to_all | solution.py:176
  201.8 8.4 %copy.63 = f32[3,32768]{0,1:T(8,128)} copy(f32[3,32768]{1,0:T(4,128)S(1)} %pad_maximum_fusion.1) | data formatting | bytes 786432 | tf_op jit(solution)/shard_map/stack | solution.py:184
  210.8 12.1 %scatter_fusion = f32[3,32768]{0,1:T(8,128)} fusion(f32[3,32768]{0,1:T(8,128)} %copy.63, s32[8]{0:T(128)S(1)} %copy-done.41, f32[8,3]{1,0:T(8,128)S(1)} %copy.64), kind=kCustom, calls=%fused_computation.1 | custom fusion | bytes 320 | tf_op jit(solution)/shard_map/scatter | solution.py:192
  223.0 30.4 %slice_reduce_fusion = (f32[32768]{0:T(1024)S(1)}, f32[32768]{0:T(1024)S(1)}, f32[32768]{0:T(1024)S(1)}) fusion(f32[3,32768]{0,1:T(8,128)} %scatter_fusion), kind=kLoop, calls=%fused_computation.3 | loop fusion | bytes 786432 | tf_op jit(solution)/shard_map/slice | solution.py:197
  254.5 1.6 collective-permute-start.5
  256.1 26.1 %collective-permute-done.5 = f32[5,1,256]{2,1,0:T(1,128)S(1)} collective-permute-done((f32[5,1,256]{2,1,0:T(1,128)S(1)}, f32[5,1,256]{2,1,0:T(1,128)S(1)}, u32[]{:S(2)}, u32[]{:S(2)}) %collective-permute-start.5) | collective-permute-done | bytes 5152 | tf_op jit(solution)/shard_map/ppermute | solution.py:27
  282.4 5.1 %collective-permute-start.7 = (f32[5,130,1]{2,1,0:T(8,128)S(1)}, f32[5,130,1]{2,1,0:T(8,128)S(1)}, u32[]{:S(2)}, u32[]{:S(2)}) collective-permute-start(f32[5,130,1]{2,1,0:T(8,128)S(1)} %get-tuple-element.26), channel_id=1, source_target_pairs={{1,0},{2,1},{3,2},{4,3},{5,4},{6,5},{7,6},{0,7},{9,8},{10,9},{11,1... | collective-permute-start | bytes 7808 | tf_op jit(solution)/shard_map/ppermute | solution.py:27
  287.8 5.2 %collective-permute-done.7 = f32[5,130,1]{2,1,0:T(8,128)S(1)} collective-permute-done((f32[5,130,1]{2,1,0:T(8,128)S(1)}, f32[5,130,1]{2,1,0:T(8,128)S(1)}, u32[]{:S(2)}, u32[]{:S(2)}) %collective-permute-start.7) | collective-permute-done | bytes 2632 | tf_op jit(solution)/shard_map/ppermute | solution.py:27
  293.0 5.4 %collective-permute-done.6 = f32[5,130,1]{2,1,0:T(8,128)S(1)} collective-permute-done((f32[5,130,1]{2,1,0:T(8,128)S(1)}, f32[5,130,1]{2,1,0:T(8,128)S(1)}, u32[]{:S(2)}, u32[]{:S(2)}) %collective-permute-start.6) | collective-permute-done | bytes 2632 | tf_op jit(solution)/shard_map/ppermute | solution.py:25
  300.6 5.2 %copy.67 = f32[16,2,3,13824]{3,1,0,2:T(2,128)} copy(f32[16,2,3,13824]{3,1,2,0:T(2,128)} %all-to-all-done) | data formatting | bytes 10616832 | tf_op jit(solution)/shard_map/all_to_all | solution.py:176
  305.9 7.0 %reshape.858 = f32[32,3,13824]{2,0,1:T(8,128)} reshape(f32[16,2,3,13824]{3,1,0,2:T(2,128)} %copy.67) | data formatting | bytes 10616832 | tf_op jit(solution)/shard_map/reshape | solution.py:183
  (231 shorter events, 52.7 us)
Async XLA Ops:
  0.6 7.3 %copy-start.14 = (f32[3,128,256]{2,1,0:T(8,128)S(1)}, f32[3,128,256]{2,1,0:T(8,128)}, u32[]{:S(2)}) copy-start(f32[3,128,256]{2,1,0:T(8,128)} %param.7) | copy-start | bytes 1179652
  0.6 6.3 %copy-start.42 = (s32[8,1]{0,1:T(1,128)S(1)}, s32[8,1]{0,1:T(1,128)}, u32[]{:S(2)}) copy-start(s32[8,1]{0,1:T(1,128)} %param.11) | copy-start | bytes 100
  1.5 6.5 %collective-permute-start.1 = (f32[3,1,256]{2,1,0:T(1,128)S(1)}, f32[3,1,256]{2,1,0:T(1,128)S(1)}, u32[]{:S(2)}, u32[]{:S(2)}) collective-permute-start(f32[3,1,256]{2,1,0:T(1,128)S(1)} %get-tuple-element.101), channel_id=1, source_target_pairs={{8,0},{16,8},{24,16},{32,24},{40,32},{48,40},{56,48},{64,56},{72,6... | collective-permute-start | bytes 9224 | tf_op jit(solution)/shard_map/ppermute | solution.py:27
  3.0 4.9 %collective-permute-start = (f32[3,1,256]{2,1,0:T(1,128)S(1)}, f32[3,1,256]{2,1,0:T(1,128)S(1)}, u32[]{:S(2)}, u32[]{:S(2)}) collective-permute-start(f32[3,1,256]{2,1,0:T(1,128)S(1)} %get-tuple-element.100), channel_id=1, source_target_pairs={{0,8},{8,16},{16,24},{24,32},{32,40},{40,48},{48,56},{56,64},{64,7... | collective-permute-start | bytes 9224 | tf_op jit(solution)/shard_map/ppermute | solution.py:25
  3.7 0.8 copy-start.40
  4.3 74.7 %copy-start.34 = (s32[576]{0:T(1024)}, s32[576]{0:T(1024)S(1)}, u32[]{:S(2)}) copy-start(s32[576]{0:T(1024)S(1)} %get-tuple-element.104) | copy-start | bytes 6916
  4.3 74.7 %copy-start.36 = (s32[576]{0:T(1024)}, s32[576]{0:T(1024)S(1)}, u32[]{:S(2)}) copy-start(s32[576]{0:T(1024)S(1)} %get-tuple-element.105) | copy-start | bytes 6916
  6.0 8.6 %copy-start = (f32[8,3,13824]{2,0,1:T(8,128)S(1)}, f32[8,3,13824]{2,0,1:T(8,128)}, u32[]{:S(2)}) copy-start(f32[8,3,13824]{2,0,1:T(8,128)} %param.12) | copy-start | bytes 3981316
  6.0 108.2 %copy-start.24 = (f32[8,3]{0,1:T(4,128)}, f32[8,3]{0,1:T(4,128)S(1)}, u32[]{:S(2)}) copy-start(f32[8,3]{0,1:T(4,128)S(1)} %broadcast_multiply_fusion.3) | copy-start | bytes 292
  7.9 43.3 %copy-start.28 = (pred[576]{0:T(1024)(128)(4,1)}, pred[576]{0:T(1024)(128)(4,1)S(1)}, u32[]{:S(2)}) copy-start(pred[576]{0:T(1024)(128)(4,1)S(1)} %get-tuple-element.102) | copy-start | bytes 1732
  7.9 43.3 %copy-start.31 = (pred[576]{0:T(1024)(128)(4,1)}, pred[576]{0:T(1024)(128)(4,1)S(1)}, u32[]{:S(2)}) copy-start(pred[576]{0:T(1024)(128)(4,1)S(1)} %get-tuple-element.103) | copy-start | bytes 1732
  8.8 6.3 %copy-start.16 = (f32[13824]{0:T(1024)S(1)}, f32[13824]{0:T(1024)}, u32[]{:S(2)}) copy-start(f32[13824]{0:T(1024)} %param.13) | copy-start | bytes 165892
  8.8 11.3 %collective-permute-start.3 = (f32[3,130,1]{2,1,0:T(8,128)}, f32[3,130,1]{2,1,0:T(8,128)}, u32[]{:S(2)}, u32[]{:S(2)}) collective-permute-start(f32[3,130,1]{2,1,0:T(8,128)} %get-tuple-element.96), channel_id=1, source_target_pairs={{1,0},{2,1},{3,2},{4,3},{5,4},{6,5},{7,6},{0,7},{9,8},{10,9},{11,1... | collective-permute-start | bytes 4688 | tf_op jit(solution)/shard_map/ppermute | solution.py:27
  14.6 11.3 %collective-permute-start.2 = (f32[3,130,1]{2,1,0:T(8,128)}, f32[3,130,1]{2,1,0:T(8,128)}, u32[]{:S(2)}, u32[]{:S(2)}) collective-permute-start(f32[3,130,1]{2,1,0:T(8,128)} %get-tuple-element.95), channel_id=1, source_target_pairs={{0,1},{1,2},{2,3},{3,4},{4,5},{5,6},{6,7},{7,0},{8,9},{9,10},{10,1... | collective-permute-start | bytes 4688 | tf_op jit(solution)/shard_map/ppermute | solution.py:25
  14.6 11.3 %copy-start.38 = (pred[258]{0:T(512)(128)(4,1)}, pred[258]{0:T(512)(128)(4,1)S(1)}, u32[]{:S(2)}) copy-start(pred[258]{0:T(512)(128)(4,1)S(1)} %fusion.196) | copy-start | bytes 778
  15.3 92.5 %copy-start.20 = (pred[13824]{0:T(1024)(128)(4,1)}, pred[13824]{0:T(1024)(128)(4,1)S(1)}, u32[]{:S(2)}) copy-start(pred[13824]{0:T(1024)(128)(4,1)S(1)} %broadcast_in_dim.120) | copy-start | bytes 41476
  15.4 92.4 %copy-start.22 = (pred[13824]{0:T(1024)(128)(4,1)}, pred[13824]{0:T(1024)(128)(4,1)S(1)}, u32[]{:S(2)}) copy-start(pred[13824]{0:T(1024)(128)(4,1)S(1)} %broadcast_in_dim.117) | copy-start | bytes 41476
  27.6 0.7 copy-start.1
  45.6 68.5 %copy-start.26 = (f32[8,3]{0,1:T(4,128)}, f32[8,3]{0,1:T(4,128)S(1)}, u32[]{:S(2)}) copy-start(f32[8,3]{0,1:T(4,128)S(1)} %copy.57) | copy-start | bytes 292
  88.3 1.7 copy-start.29
  88.3 1.7 copy-start.32
  107.8 1.7 copy-start.4
  107.8 1.7 copy-start.6
  109.5 0.8 copy-start.8
  157.9 1.0 copy-start.2
  157.9 1.0 copy-start.18
  169.0 2.8 copy-start.21
  169.0 2.8 copy-start.23
  170.8 2.7 copy-start.25
  170.8 2.7 copy-start.27
  171.8 1.8 copy-start.5
  171.8 1.8 copy-start.7
  171.8 1.8 copy-start.9
  171.8 1.9 copy-start.11
  171.8 2.1 copy-start.12
  177.2 3.7 %copy-start.43 = (s32[8]{0:T(128)S(1)}, s32[8]{0:T(128)}, u32[]{:S(2)}) copy-start(s32[8]{0:T(128)} %fusion.199) | copy-start | bytes 100
  194.7 5.9 %copy-start.15 = (f32[1,1,128,256]{3,1,2,0:T(1,128)S(1)}, f32[1,1,128,256]{3,1,2,0:T(1,128)}, u32[]{:S(2)}) copy-start(f32[1,1,128,256]{3,1,2,0:T(1,128)} %copy.68) | copy-start | bytes 393220
  194.7 6.3 %copy-start.10 = (f32[8,13824]{1,0:T(8,128)S(1)}, f32[8,13824]{1,0:T(8,128)}, u32[]{:S(2)}) copy-start(f32[8,13824]{1,0:T(8,128)} %get-tuple-element.5) | copy-start | bytes 1327108
  194.7 6.3 %copy-start.17 = (f32[13824]{0:T(1024)S(1)}, f32[13824]{0:T(1024)}, u32[]{:S(2)}) copy-start(f32[13824]{0:T(1024)} %param.13) | copy-start | bytes 165892
  194.7 105.9 %all-to-all-start = ((f32[16,2,3,13824]{3,1,2,0:T(2,128)}), f32[16,2,3,13824]{3,1,2,0:T(2,128)}, u32[]{:S(2)}, u32[]{:S(2)}) async-start(f32[16,2,3,13824]{3,1,2,0:T(2,128)} %copy.66), calls=%async_computation | async-start | bytes 10616832 | tf_op jit(solution)/shard_map/all_to_all | solution.py:176
  201.8 8.4 %copy-start.13 = (f32[8,13824]{1,0:T(8,128)S(1)}, f32[8,13824]{1,0:T(8,128)}, u32[]{:S(2)}) copy-start(f32[8,13824]{1,0:T(8,128)} %add_multiply_fusion) | copy-start | bytes 1327108
  253.4 1.0 copy-start.3
  254.5 43.9 %copy-start.39 = (pred[258]{0:T(512)(128)(4,1)S(1)}, pred[258]{0:T(512)(128)(4,1)}, u32[]{:S(2)}) copy-start(pred[258]{0:T(512)(128)(4,1)} %copy-done.38) | copy-start | bytes 778
  254.5 27.6 %collective-permute-start.5 = (f32[5,1,256]{2,1,0:T(1,128)S(1)}, f32[5,1,256]{2,1,0:T(1,128)S(1)}, u32[]{:S(2)}, u32[]{:S(2)}) collective-permute-start(f32[5,1,256]{2,1,0:T(1,128)S(1)} %get-tuple-element.28), channel_id=1, source_target_pairs={{8,0},{16,8},{24,16},{32,24},{40,32},{48,40},{56,48},{64,56},{72,6... | collective-permute-start | bytes 15368 | tf_op jit(solution)/shard_map/ppermute | solution.py:27
  256.1 26.1 %collective-permute-start.4 = (f32[5,1,256]{2,1,0:T(1,128)S(1)}, f32[5,1,256]{2,1,0:T(1,128)S(1)}, u32[]{:S(2)}, u32[]{:S(2)}) collective-permute-start(f32[5,1,256]{2,1,0:T(1,128)S(1)} %get-tuple-element.27), channel_id=1, source_target_pairs={{0,8},{8,16},{16,24},{24,32},{32,40},{40,48},{48,56},{56,64},{64,7... | collective-permute-start | bytes 15368 | tf_op jit(solution)/shard_map/ppermute | solution.py:25
  282.4 10.6 %collective-permute-start.7 = (f32[5,130,1]{2,1,0:T(8,128)S(1)}, f32[5,130,1]{2,1,0:T(8,128)S(1)}, u32[]{:S(2)}, u32[]{:S(2)}) collective-permute-start(f32[5,130,1]{2,1,0:T(8,128)S(1)} %get-tuple-element.26), channel_id=1, source_target_pairs={{1,0},{2,1},{3,2},{4,3},{5,4},{6,5},{7,6},{0,7},{9,8},{10,9},{11,1... | collective-permute-start | bytes 7808 | tf_op jit(solution)/shard_map/ppermute | solution.py:27
  287.5 10.9 %collective-permute-start.6 = (f32[5,130,1]{2,1,0:T(8,128)S(1)}, f32[5,130,1]{2,1,0:T(8,128)S(1)}, u32[]{:S(2)}, u32[]{:S(2)}) collective-permute-start(f32[5,130,1]{2,1,0:T(8,128)S(1)} %get-tuple-element.25), channel_id=1, source_target_pairs={{0,1},{1,2},{2,3},{3,4},{4,5},{5,6},{6,7},{7,0},{8,9},{9,10},{10,1... | collective-permute-start | bytes 7808 | tf_op jit(solution)/shard_map/ppermute | solution.py:25
  298.9 0.9 copy-start.19
  (5 other events, 3.3 us)
where the time goes:
time: 319 us; the launch traced here: 313 us
  local copies, waits for them, and re-layouts  140 us (44%)
  matrix products  69.3 us (22%)
  waiting for transfers between devices  47.2 us (15%)
  other arithmetic  34.8 us (11%)
  starting transfers between devices  20.2 us (6%)
    dot_general x8, matrix products, plane_product(): return jnp.einsum('nxp,pq->nxq', values, table, precision=HIGHEST)  59.6 us
    ppermute x4, waiting for transfers between devices, padded_2(): lax.ppermute(head, axis, [((i + 1) % count, i) for i in range(count)])  35.9 us
    slice x2, local copies, waits for them, and re-layouts, local(): stress[1]  30.5 us
    ppermute x4, starting transfers between devices, padded_2(): lax.ppermute(head, axis, [((i + 1) % count, i) for i in range(count)])  14 us
    scatter x1, local copies, waits for them, and re-layouts, local(): stress.reshape(3, -1).at[:, yield_points].set(point_stress.T)  12.1 us
    ppermute x4, waiting for transfers between devices, padded_2(): lax.ppermute(tail, axis, [(i, (i + 1) % count) for i in range(count)])  11.2 us
    dot_general x16, matrix products, line_product(): return jnp.einsum('kx,nxq->nkq', table, values, precision=HIGHEST)  9.68 us
    another operation x1, local copies, waits for them, and re-layouts, local(): jnp.stack([gore_slope[0] + 0.5 * gore_slope[2] * gore_slope[2], band_slop...  9.18 us
  transfers between devices with their start and end apart: 9, of which 5 were waited for; matrix products, arithmetic and copies ran while one was open for 19% of the time, Pallas kernels for 0%

commit v1 on v0

v1 whole, which is shorter than its diff:
```python
import math

import jax
import jax.numpy as jnp
import numpy as np
from jax import lax
from jax.experimental import pallas as pl
from jax.experimental.pallas import tpu as pltpu
from jax.sharding import PartitionSpec as P

G = 24
PLANE = G * G
VOX = G * G * G
SWEEPS = 2
POISSON = 0.3
CAP = 8
MOST = 2
ROWS = 3 * VOX // 128
PACK = 328
MESH = pl.DeviceIdType.MESH
F32 = jnp.float32
BF16 = jnp.bfloat16


def tables():
    n = np.arange(G)
    phase = 2.0 * np.pi * (np.outer(n, n) % G) / G
    hartley = (np.cos(phase) + np.sin(phase)) / math.sqrt(G)
    plane = np.kron(hartley, hartley)
    line = np.kron(hartley, np.eye(CAP))

    def split(a):
        high = a.astype(np.float32).astype(jnp.bfloat16)
        low = (a - high.astype(np.float64)).astype(np.float32).astype(jnp.bfloat16)
        return high, low

    square = np.sin(phase[1]) ** 2
    summed = square[:, None, None] + square[None, :, None] + square[None, None, :]
    level = n % (G // 2) == 0
    silent = level[:, None, None] & level[None, :, None] & level[None, None, :]
    weight = np.where(silent, 0.0, 1.0 / (10.0 * np.where(silent, 1.0, summed)))
    plane_high, plane_low = split(plane)
    line_high, line_low = split(line)
    return (
        plane_high,
        plane_low,
        np.concatenate([line_high, line_low], axis=0),
        weight.reshape(G, 1, PLANE).astype(np.float32),
    )


def shifted(v, k):
    k = k % v.shape[1]
    return jnp.concatenate([v[:, k:], v[:, :k]], axis=1)


def diff_upper(v):
    return shifted(v, G) - shifted(v, -G)


def diff_lower(v, low):
    forward = jnp.where(low == G - 1, shifted(v, 1 - G), shifted(v, 1))
    backward = jnp.where(low == 0, shifted(v, G - 1), shifted(v, -1))
    return forward - backward


def to_row(column):
    n = column.shape[0]
    diagonal = lax.broadcasted_iota(jnp.int32, (n, n), 0) == lax.broadcasted_iota(jnp.int32, (n, n), 1)
    return jnp.sum(jnp.where(diagonal, column, 0.0), axis=0, keepdims=True)


def to_column(row):
    n = row.shape[1]
    diagonal = lax.broadcasted_iota(jnp.int32, (n, n), 0) == lax.broadcasted_iota(jnp.int32, (n, n), 1)
    return jnp.sum(jnp.where(diagonal, row, 0.0), axis=1, keepdims=True)


def gore_diff(v, before, after):
    down = jnp.concatenate([v[1:], after], axis=0)
    up = jnp.concatenate([before, v[:-1]], axis=0)
    return (down - up) * 0.5


def band_diff(v, before, after):
    right = jnp.concatenate([v[:, 1:], after], axis=1)
    left = jnp.concatenate([before, v[:, :-1]], axis=1)
    return (right - left) * 0.5


def kernel(
    n_gore, n_band,
    yield_ref, route_ref, disp_ref, stiff_ref, press_ref, state_ref, weave_ref,
    plane_hi_ref, plane_lo_ref, line_ref, weight_ref,
    force_ref, recv_ref,
    halo_g, halo_b, got_g, got_b, slopes, strain_s,
    e_s, s_pad, d_s, x_s, f_s, cells, send,
    halo_send, halo_recv, send_sem, recv_sem, own_sem,
):
    g, b = lax.axis_index("gore"), lax.axis_index("band")
    up, down = lax.rem(g + 1, n_gore), lax.rem(g + n_gore - 1, n_gore)
    right, left = lax.rem(b + 1, n_band), lax.rem(b + n_band - 1, n_band)
    nodes_g, nodes_b = stiff_ref.shape

    barrier = pltpu.get_barrier_semaphore()
    for d in range(1, n_gore):
        pl.semaphore_signal(barrier, inc=1, device_id=(lax.rem(g + d, n_gore), b), device_id_type=MESH)
    pl.semaphore_signal(barrier, inc=1, device_id=(g, right), device_id_type=MESH)
    pl.semaphore_signal(barrier, inc=1, device_id=(g, left), device_id_type=MESH)

    def halo_copies(k):
        out = []
        for side, target in enumerate(((down, b), (up, b), (g, left), (g, right))):
            source, place = (halo_g, got_g) if side < 2 else (halo_b, got_b)
            out.append(
                pltpu.make_async_remote_copy(
                    src_ref=source.at[2 * k + side % 2],
                    dst_ref=place.at[2 * k + side % 2],
                    send_sem=halo_send.at[4 * k + side],
                    recv_sem=halo_recv.at[4 * k + side],
                    device_id=target,
                    device_id_type=MESH,
                )
            )
        return out

    for c in range(3):
        v = disp_ref[c]
        halo_g[0, c : c + 1, :] = v[0:1]
        halo_g[1, c : c + 1, :] = v[nodes_g - 1 :]
        halo_b[0, c : c + 1, :] = to_row(v[:, 0:1])
        halo_b[1, c : c + 1, :] = to_row(v[:, nodes_b - 1 :])
    pl.semaphore_wait(barrier, n_gore + 1)
    first = halo_copies(0)
    for copy in first:
        copy.start()

    def load_states(i, sums):
        out = []
        for c in range(3):
            pair = state_ref[c, :, pl.ds(pl.multiple_of(i * 2 * PLANE, 128), 2 * PLANE)]
            even, odd = pair[:, :PLANE], pair[:, PLANE:]
            e_s[c, pl.ds(pl.multiple_of(i * 16, 16), 16), :] = jnp.concatenate([even, odd], axis=0)
            out.append(sums[c] + even + odd)
        return tuple(out)

    zero = jnp.zeros((CAP, PLANE), F32)
    sums = lax.fori_loop(0, G // 2, load_states, (zero, zero, zero))
    means = [jnp.sum(s, axis=1, keepdims=True) * (1.0 / VOX) for s in sums]

    for copy in first:
        copy.wait()

    inner_left, inner_right = b > 0, b < n_band - 1
    for c in range(3):
        v = disp_ref[c]
        before = jnp.where(inner_left, to_column(got_b[1, c : c + 1, :]), 0.0)
        after = jnp.where(inner_right, to_column(got_b[0, c : c + 1, :]), 0.0)
        slopes[c] = gore_diff(v, got_g[1, c : c + 1, :], got_g[0, c : c + 1, :])
        slopes[3 + c] = band_diff(v, before, after)
    gz, bz = slopes[2], slopes[5]
    strain_s[0] = slopes[0] + 0.5 * gz * gz
    strain_s[1] = slopes[4] + 0.5 * bz * bz
    strain_s[2] = 0.5 * (slopes[3] + slopes[1]) + 0.5 * gz * bz

    cell_row = lax.broadcasted_iota(jnp.int32, (CAP, 1), 0)
    lane = lax.broadcasted_iota(jnp.int32, (CAP, nodes_b), 1)
    points = [yield_ref[r] for r in range(CAP)]
    wanted = jnp.zeros((CAP, 1), jnp.int32)
    for r in range(CAP):
        wanted = jnp.where(cell_row == r, lax.rem(points[r], nodes_b), wanted)
    shift = []
    for c in range(3):
        rows = [strain_s[c, pl.ds(lax.div(points[r], nodes_b), 1), :] for r in range(CAP)]
        rows = jnp.concatenate(rows, axis=0)
        drive = jnp.sum(jnp.where(lane == wanted, rows, 0.0), axis=1, keepdims=True)
        drive = drive - means[c]
        shift.append(jnp.concatenate([drive, drive], axis=0))

    low = lax.rem(lax.broadcasted_iota(jnp.int32, (16, PLANE), 1), G)

    def stiffness_of(i):
        even = jnp.broadcast_to(weave_ref[2 * i], (CAP, PLANE))
        odd = jnp.broadcast_to(weave_ref[2 * i + 1], (CAP, PLANE))
        return jnp.concatenate([even, odd], axis=0)

    def advance(i, sweep):
        at = pl.multiple_of(i * 16, 16)
        e = [e_s[c, pl.ds(at, 16), :] for c in range(3)]
        if sweep == 0:
            e = [e[c] + shift[c] for c in range(3)]
        else:
            middle = f_s[pl.ds(at + 8, 16), :]
            e[0] = e[0] + 0.5 * (f_s[pl.ds(at + 16, 16), :] - f_s[pl.ds(at, 16), :])
            e[1] = e[1] + 0.5 * diff_upper(middle)
            e[2] = e[2] + 0.5 * diff_lower(middle, low)
        size = e[0] * e[0] + e[1] * e[1] + e[2] * e[2]
        factor = stiffness_of(i) * (1.5 - 0.5 / (1.0 + size))
        return at, e, [factor * v for v in e]

    def parts(v):
        high = v.astype(BF16)
        return high, (v - high.astype(F32)).astype(BF16)

    def lines(v):
        high, rest = parts(v)
        both = jnp.dot(line_ref[...], high, preferred_element_type=F32)
        n = G * CAP
        return both[:n] + both[n:] + jnp.dot(line_ref[0:n, :], rest, preferred_element_type=F32)

    def planes(both):
        n = G * CAP
        out = jnp.dot(both, plane_hi_ref[...], preferred_element_type=F32)
        return out[:n] + out[n:] + jnp.dot(both[:n], plane_lo_ref[...], preferred_element_type=F32)

    for sweep in range(SWEEPS):

        def law(i, carry, sweep=sweep):
            at, e, s = advance(i, sweep)
            for c in range(3):
                e_s[c, pl.ds(at, 16), :] = e[c]
            s_pad[pl.ds(at + 8, 16), :] = s[0]
            d_s[pl.ds(at, 16), :] = diff_upper(s[1]) + diff_lower(s[2], low)
            return carry

        lax.fori_loop(0, G // 2, law, 0)
        s_pad[0:8, :] = s_pad[G * 8 : G * 8 + 8, :]
        s_pad[G * 8 + 8 :, :] = s_pad[8:16, :]

        def source(i, carry):
            at = pl.multiple_of(i * 16, 16)
            v = 0.5 * (s_pad[pl.ds(at + 16, 16), :] - s_pad[pl.ds(at, 16), :] + d_s[pl.ds(at, 16), :])
            high, rest = parts(v)
            x_s[pl.ds(at, 16), :] = high
            x_s[pl.ds(G * CAP + at, 16), :] = rest
            return carry

        lax.fori_loop(0, G // 2, source, 0)
        spectrum = lines(planes(x_s[...]))
        weight = jnp.broadcast_to(weight_ref[...], (G, CAP, PLANE)).reshape(G * CAP, PLANE)
        back = lines(spectrum * weight)
        high, rest = parts(back)
        x_s[0 : G * CAP, :] = high
        x_s[G * CAP :, :] = rest
        f_s[8 : G * 8 + 8, :] = planes(x_s[...])
        f_s[0:8, :] = f_s[G * 8 : G * 8 + 8, :]
        f_s[G * 8 + 8 :, :] = f_s[8:16, :]

    def finish(i, sums):
        at, e, s = advance(i, SWEEPS)
        out = []
        for c in range(3):
            wide = jnp.concatenate([e[c][0:8], e[c][8:16]], axis=1)
            for t in range(2 * PLANE // 128):
                row = pl.multiple_of((c * (VOX // 128) + i * 9 + t) * CAP, CAP)
                cells[pl.ds(row, CAP), :] = wide[:, 128 * t : 128 * t + 128]
            out.append(sums[c] + s[c][0:8] + s[c][8:16])
        return tuple(out)

    sums = lax.fori_loop(0, G // 2, finish, (zero, zero, zero))
    point_stress = [jnp.sum(s, axis=1, keepdims=True) * (1.0 / VOX) for s in sums]

    stiff = stiff_ref[...]
    e11, e22, e12 = strain_s[0], strain_s[1], strain_s[2]
    stress = [
        stiff * (e11 + POISSON * e22),
        stiff * (e22 + POISSON * e11),
        stiff * (1.0 - POISSON) * e12,
    ]
    node = lax.broadcasted_iota(jnp.int32, stiff.shape, 0) * nodes_b + lax.broadcasted_iota(jnp.int32, stiff.shape, 1)
    for r in range(CAP):
        here = node == points[r]
        for c in range(3):
            stress[c] = jnp.where(here, point_stress[c][r : r + 1, :], stress[c])
    s11, s22, s12 = stress
    gz, bz = slopes[2], slopes[5]
    t1 = s11 * gz + s12 * bz
    t2 = s12 * gz + s22 * bz
    over_gore, over_band = [s11, s12, t1], [s12, s22, t2]
    for c in range(3):
        halo_g[2, c : c + 1, :] = over_gore[c][0:1]
        halo_g[3, c : c + 1, :] = over_gore[c][nodes_g - 1 :]
        halo_b[2, c : c + 1, :] = to_row(over_band[c][:, 0:1])
        halo_b[3, c : c + 1, :] = to_row(over_band[c][:, nodes_b - 1 :])
    second = halo_copies(1)
    for copy in second:
        copy.start()
    slopes[0] = s11
    slopes[1] = s12
    slopes[3] = s22
    slopes[4] = t1
    slopes[5] = t2

    workers = [route_ref[r] for r in range(CAP)]

    def slot_copy(d):
        return pltpu.make_async_remote_copy(
            src_ref=send.at[d],
            dst_ref=recv_ref.at[g],
            send_sem=send_sem.at[d],
            recv_sem=recv_sem.at[d],
            device_id=(lax.rem(g + d, n_gore), b),
            device_id_type=MESH,
        )

    def pack(d):
        worker = lax.rem(g + d, n_gore)
        one, two = jnp.int32(CAP), jnp.int32(CAP)
        for r in reversed(range(CAP)):
            named = workers[r] == worker
            two = jnp.where(named, one, two)
            one = jnp.where(named, r, one)
        for k, cell in enumerate((one, two)):
            filled = cell < CAP
            begin = lax.rem(cell, CAP)

            def rows(m, carry):
                v = cells[pl.ds(m * 64 + begin, 8, stride=CAP), :]
                send[d, k, pl.ds(pl.multiple_of(m * 8, 8), 8), :] = jnp.where(filled, v, 0.0)
                return carry

            lax.fori_loop(0, PACK // 8, rows, 0, unroll=True)

    cells[ROWS * CAP :, :] = jnp.zeros((PACK * CAP - ROWS * CAP, 128), F32)

    def dispatch(d, carry):
        pack(d)
        slot_copy(d).start()
        return carry

    lax.fori_loop(1, n_gore, dispatch, 0)
    pack(0)
    own = pltpu.make_async_copy(send.at[0], recv_ref.at[g], own_sem)
    own.start()

    for copy in second:
        copy.wait()
    edge = []
    for c in range(3):
        before = jnp.where(inner_left, to_column(got_b[3, c : c + 1, :]), 0.0)
        after = jnp.where(inner_right, to_column(got_b[2, c : c + 1, :]), 0.0)
        edge.append((before, after))
    pairs = ((0, 1), (1, 3), (4, 5))
    for c, (p, q) in enumerate(pairs):
        value = gore_diff(slopes[p], got_g[3, c : c + 1, :], got_g[2, c : c + 1, :])
        value = value + band_diff(slopes[q], *edge[c])
        if c == 2:
            value = value + press_ref[...]
        force_ref[c] = value

    own.wait()

    def settle(d, carry):
        copy = slot_copy(d)
        copy.wait_send()
        copy.wait_recv()
        return carry

    lax.fori_loop(1, n_gore, settle, 0)


def layout_kernel(slots, recv_ref, out_ref, got, made, in_sem, out_sem):
    tiles = VOX // 128
    spans = []
    for c in range(3):
        low = c * tiles // 8 * 8
        high = min(-(-(c + 1) * tiles // 8) * 8, PACK)
        spans.append((low, high))
    loads = []
    for c, (low, high) in enumerate(spans):
        place = got.at[c, :, 0 : high - low, :]
        loads.append(pltpu.make_async_copy(recv_ref.at[:, low:high, :], place, in_sem.at[c]))
        loads[-1].start()
    stores = []
    for c, (low, _) in enumerate(spans):
        loads[c].wait()
        for t in range(slots // 8):

            def column(j, carry):
                v = got[c, 8 * t : 8 * t + 8, pl.ds(c * tiles - low + 4 * j, 4), :]
                for s in range(4):
                    made[c, 8 * t : 8 * t + 8, pl.ds(pl.multiple_of((4 * j + s) * 128, 128), 128)] = v[:, s, :]
                return carry

            lax.fori_loop(0, tiles // 4, column, 0)
        stores.append(pltpu.make_async_copy(made.at[c], out_ref.at[c], out_sem.at[c]))
        stores[-1].start()
    for copy in stores:
        copy.wait()


def local(displacement, stiffness, pressure, yield_points, route, cell_state, weave):
    n_gore, n_band = lax.axis_size("gore"), lax.axis_size("band")
    slots = n_gore * MOST
    nodes_g, nodes_b = stiffness.shape
    plane_high, plane_low, line, weight = tables()
    vmem, smem = pl.BlockSpec(memory_space=pltpu.VMEM), pl.BlockSpec(memory_space=pltpu.SMEM)
    any_space = pl.BlockSpec(memory_space=pl.ANY)
    n = G * CAP

    def run(*args):
        return pl.pallas_call(
            lambda *refs: kernel(n_gore, n_band, *refs),
            out_shape=(
                jax.ShapeDtypeStruct((3, nodes_g, nodes_b), F32),
                jax.ShapeDtypeStruct((n_gore, MOST, PACK, 128), F32),
            ),
            in_specs=[smem, smem] + [vmem] * 9,
            out_specs=(vmem, any_space),
            scratch_shapes=[
                pltpu.VMEM((4, 8, nodes_b), F32),
                pltpu.VMEM((4, 8, nodes_g), F32),
                pltpu.VMEM((4, 8, nodes_b), F32),
                pltpu.VMEM((4, 8, nodes_g), F32),
                pltpu.VMEM((6, nodes_g, nodes_b), F32),
                pltpu.VMEM((3, nodes_g, nodes_b), F32),
                pltpu.VMEM((3, n, PLANE), F32),
                pltpu.VMEM((n + 16, PLANE), F32),
                pltpu.VMEM((n, PLANE), F32),
                pltpu.VMEM((2 * n, PLANE), BF16),
                pltpu.VMEM((n + 16, PLANE), F32),
                pltpu.VMEM((PACK * CAP, 128), F32),
                pltpu.VMEM((n_gore, MOST, PACK, 128), F32),
                pltpu.SemaphoreType.DMA((8,)),
                pltpu.SemaphoreType.DMA((8,)),
                pltpu.SemaphoreType.DMA((n_gore,)),
                pltpu.SemaphoreType.DMA((n_gore,)),
                pltpu.SemaphoreType.DMA,
            ],
            compiler_params=pltpu.CompilerParams(
                collective_id=0, has_side_effects=True, vmem_limit_bytes=48 * 2**20
            ),
            name="cells",
        )(*args)

    force, recv = run(
        yield_points,
        route.reshape(-1),
        displacement,
        stiffness,
        pressure,
        cell_state.transpose(1, 0, 2),
        weave.reshape(G, 1, PLANE),
        jnp.asarray(plane_high),
        jnp.asarray(plane_low),
        jnp.asarray(line),
        jnp.asarray(weight),
    )
    cell_strain = pl.pallas_call(
        lambda *refs: layout_kernel(slots, *refs),
        out_shape=jax.ShapeDtypeStruct((3, slots, VOX), F32),
        in_specs=[any_space],
        out_specs=any_space,
        scratch_shapes=[
            pltpu.VMEM((3, slots, 120, 128), F32),
            pltpu.VMEM((3, slots, VOX), F32),
            pltpu.SemaphoreType.DMA((3,)),
            pltpu.SemaphoreType.DMA((3,)),
        ],
        compiler_params=pltpu.CompilerParams(vmem_limit_bytes=32 * 2**20),
        name="layout",
    )(recv.reshape(slots, PACK, 128))
    return force, cell_strain.transpose(1, 0, 2)


def solution(mesh):
    return jax.shard_map(
        local,
        mesh=mesh,
        in_specs=(
            P(None, "gore", "band"),
            P("gore", "band"),
            P("gore", "band"),
            P(("gore", "band")),
            P(("gore", "band"), None),
            P(("gore", "band"), None, None),
            P(),
        ),
        out_specs=(P(None, "gore", "band"), P(("gore", "band"), None, None)),
        check_vma=False,
    )
```

time: 319 us -> 138 us (0.43)
  the two profiles are of different devices: /device:TPU:24 before, /device:TPU:49 now
where the time goes in v1:
time: 138 us
  Pallas kernels  123 us (89%)
  local copies, waits for them, and re-layouts  13.6 us (10%)
    pallas_call x1, Pallas kernels, run(): pl.pallas_call(lambda *refs: kernel(n_gore, n_band, *refs), out_shape=(ja...  117 us
    unnamed x23, local copies, waits for them, and re-layouts  12.7 us
    pallas_call x1, Pallas kernels, local(): pl.pallas_call(lambda *refs: layout_kernel(slots, *refs), out_shape=jax.S...  5.89 us

profile of v1, /device:TPU:49, one launch (start us, length us, event | category | flops | bytes accessed | tf_op | source)
XLA Modules:
  0.0 137.6 jit_solution(16870156849803651297)
XLA Ops:
  0.6 0.9 reshape.14.refs_6_
  1.6 0.0 copy-start.1
  1.6 1.3 copy-done.1
  2.9 0.0 copy-start.2
  2.9 1.1 copy-done.2
  4.0 0.0 copy-start.3
  4.0 1.1 copy-done.3
  5.1 0.0 copy-start.4
  5.1 1.0 copy-done.4
  6.1 0.0 copy-start.5
  6.1 0.9 copy-done.5
  7.0 0.0 copy-start.6
  7.0 0.9 copy-done.6
  7.9 0.0 copy-start.7
  7.9 0.9 copy-done.7
  8.9 0.0 copy-start.8
  8.9 0.8 copy-done.8
  9.7 0.0 copy-start.9
  9.7 0.7 copy-done.9
  10.3 0.0 copy-start.10
  10.3 0.7 copy-done.10
  11.0 117.4 %cells.1 = (f32[3,128,256]{2,1,0:T(8,128)S(1)}, f32[16,2,328,128]{3,2,1,0:T(8,128)}) custom-call(s32[8]{0:T(128)S(1)} %copy-done.9, s32[8]{0:T(128)S(1)} %bitcast.6, f32[3,128,256]{2,1,0:T(8,128)S(1)} %copy-done.4, f32[128,256]{1,0:T(8,128)S(1)} %copy-done.6, f32[128,256]{1,0:T(8,128)S(1)} %copy-done.7, f32[3,8,13824]{2,1,0:T(8,128)S(1)} %bitcast.5, ...), custom_call_target="tpu_custom_call" | custom-call | tf_op jit(solution)/shard_map/cells/pallas_call | solution.py:402
  128.4 0.0 copy-start
  128.4 2.5 %copy-done = f32[16,2,328,128]{3,2,1,0:T(8,128)S(1)} copy-done((f32[16,2,328,128]{3,2,1,0:T(8,128)S(1)}, f32[16,2,328,128]{3,2,1,0:T(8,128)}, u32[]{:S(2)}) %copy-start) | copy-done | bytes 5373976
  130.9 5.9 %layout.1 = f32[3,32,13824]{2,1,0:T(8,128)} custom-call(f32[32,328,128]{2,1,0:T(8,128)S(1)} %bitcast.4), custom_call_target="tpu_custom_call" | custom-call | tf_op jit(solution)/shard_map/layout/pallas_call | solution.py:449
  136.8 0.7 copy.14
Async XLA Ops:
  1.6 1.3 copy-start.1
  2.9 1.1 copy-start.2
  4.0 1.1 copy-start.3
  5.1 1.0 copy-start.4
  6.1 0.9 copy-start.5
  7.0 0.9 copy-start.6
  7.9 0.9 copy-start.7
  8.9 0.8 copy-start.8
  9.7 0.7 copy-start.9
  10.3 0.7 copy-start.10
  128.4 2.5 %copy-start = (f32[16,2,328,128]{3,2,1,0:T(8,128)S(1)}, f32[16,2,328,128]{3,2,1,0:T(8,128)}, u32[]{:S(2)}) copy-start(f32[16,2,328,128]{3,2,1,0:T(8,128)} %get-tuple-element.5) | copy-start | bytes 16121860

commit v2 on v1

--- a/solution.py
+++ b/solution.py
@@ -17,6 +17,13 @@
 MOST = 2
 ROWS = 3 * VOX // 128
 PACK = 328
+RING, LINE, CORE = 4, 2, 2
+GROUP = RING * LINE * CORE
+RING_FIRST, LINE_SECOND, LINE_FIRST, RING_SECOND = 5, 10, 8, 6
+STEPS = (1, 3, 2)
+FINAL_RING = RING * RING_FIRST
+FINAL_LINE = FINAL_RING + LINE_SECOND
+FINAL = FINAL_LINE + RING * RING_SECOND
 MESH = pl.DeviceIdType.MESH
 F32 = jnp.float32
 BF16 = jnp.bfloat16
@@ -88,16 +95,75 @@
     return (right - left) * 0.5
 
 
+def rank_of(key, key_column, earlier):
+    return jnp.sum(jnp.where((key_column == key) & earlier, 1.0, 0.0), axis=0, keepdims=True)
+
+
+def routing(worker, g):
+    n = GROUP * CAP
+    lane = lax.broadcasted_iota(jnp.int32, (1, n), 1)
+    to = worker.astype(jnp.int32)
+    source = lane >> 3
+    to_y, to_z = to >> 2, (to >> 1) & 1
+    from_y, from_z, from_c = source >> 2, (source >> 1) & 1, source & 1
+    y, z, c = g >> 2, (g >> 1) & 1, g & 1
+    crossing, first = to_z != from_z, from_c == 0
+    alone = -1 - lane
+    earlier = lax.broadcasted_iota(jnp.int32, (n, n), 0) < lax.broadcasted_iota(jnp.int32, (n, n), 1)
+
+    def rank(key):
+        key = key.astype(F32)
+        return rank_of(key, to_column(key), earlier).astype(jnp.int32)
+
+    ring_first = rank(source * RING + to_y)
+    line_second = rank(jnp.where(first & crossing, from_z * RING + to_y, alone))
+    line_first = rank(jnp.where(crossing, source, alone))
+    ring_second = rank(jnp.where(first, alone, (from_y * RING + to_y) * LINE + to_z))
+    slot = rank(source * GROUP + to)
+    over = first & ((ring_first >= RING_FIRST) | (crossing & (line_second >= LINE_SECOND)))
+    over = over | (jnp.logical_not(first) & (ring_second >= RING_SECOND))
+
+    own, mine = source == g, from_c == c
+    at_ring = c == 0
+    cell = lane & 7
+    place1_ring = jnp.where(own, to_y * RING_FIRST + ring_first, -1)
+    place1 = jnp.where(at_ring, place1_ring, jnp.where(own & crossing, line_first, -1))
+    place2_ring = jnp.where(mine & crossing & (from_z == z) & (to_y == y), line_second, -1)
+    place2_line = jnp.where(mine & (from_y == y) & (to_z == z), to_y * RING_SECOND + ring_second, -1)
+    place2 = jnp.where(at_ring, place2_ring, place2_line)
+    from_ring = from_y * RING_FIRST + ring_first
+    from_line = jnp.where(from_z == z, cell, CAP + line_first)
+    index2 = jnp.where(at_ring, from_ring, from_line)
+    place3 = jnp.where(to == g, source * MOST + slot, -1)
+    index3 = jnp.where(crossing, FINAL_RING + line_second, from_ring)
+    index3 = jnp.where(first, index3, FINAL_LINE + from_y * RING_SECOND + ring_second)
+
+    column = lax.broadcasted_iota(jnp.int32, (n, n), 1).astype(F32)
+
+    def listing(place, index):
+        place, index = to_column(place.astype(F32)), to_column(index.astype(F32) + 1.0)
+        return jnp.sum(jnp.where(place == column, index, 0.0), axis=0, keepdims=True).astype(jnp.int32)
+
+    over = jnp.sum(jnp.where(over, 1.0, 0.0), axis=1, keepdims=True)
+    return listing(place1, cell), listing(place2, index2), listing(place3, index3), over
+
+
 def kernel(
     n_gore, n_band,
+    yield_hbm, route_hbm, disp_hbm, stiff_hbm, press_hbm, state_hbm, weave_hbm,
+    plane_hi_hbm, plane_lo_hbm, line_hbm, weight_hbm,
+    force_ref, flag_ref, result_ref, own_ref,
     yield_ref, route_ref, disp_ref, stiff_ref, press_ref, state_ref, weave_ref,
     plane_hi_ref, plane_lo_ref, line_ref, weight_ref,
-    force_ref, recv_ref,
     halo_g, halo_b, got_g, got_b, slopes, strain_s,
-    e_s, s_pad, d_s, x_s, f_s, cells, send,
-    halo_send, halo_recv, send_sem, recv_sem, own_sem,
+    e_s, w_s, s_pad, d_s, x_s, f_s, cells,
+    names, names_got, flag, flag_got, table_v, table,
+    own, send1, send2, ring_got, line_got, final, chosen,
+    in_sem, halo_send, halo_recv, name_send, name_recv, flag_send, flag_recv, table_sem,
+    hop1_send, hop1_recv, hop2_send, hop2_recv, share_send, share_recv, local_sem, out_sem,
 ):
     g, b = lax.axis_index("gore"), lax.axis_index("band")
+    y, z, core = lax.div(g, LINE * CORE), lax.rem(lax.div(g, CORE), LINE), lax.rem(g, CORE)
     up, down = lax.rem(g + 1, n_gore), lax.rem(g + n_gore - 1, n_gore)
     right, left = lax.rem(b + 1, n_band), lax.rem(b + n_band - 1, n_band)
     nodes_g, nodes_b = stiff_ref.shape
@@ -105,8 +171,17 @@
     barrier = pltpu.get_barrier_semaphore()
     for d in range(1, n_gore):
         pl.semaphore_signal(barrier, inc=1, device_id=(lax.rem(g + d, n_gore), b), device_id_type=MESH)
-    pl.semaphore_signal(barrier, inc=1, device_id=(g, right), device_id_type=MESH)
-    pl.semaphore_signal(barrier, inc=1, device_id=(g, left), device_id_type=MESH)
+    for d in range(1, n_band):
+        pl.semaphore_signal(barrier, inc=1, device_id=(g, lax.rem(b + d, n_band)), device_id_type=MESH)
+
+    operands = (
+        (route_hbm, route_ref), (disp_hbm, disp_ref), (yield_hbm, yield_ref), (state_hbm, state_ref),
+        (weave_hbm, weave_ref), (stiff_hbm, stiff_ref), (plane_hi_hbm, plane_hi_ref),
+        (plane_lo_hbm, plane_lo_ref), (line_hbm, line_ref), (weight_hbm, weight_ref), (press_hbm, press_ref),
+    )
+    loads = [pltpu.make_async_copy(p, q, in_sem.at[i]) for i, (p, q) in enumerate(operands)]
+    for copy in loads:
+        copy.start()
 
     def halo_copies(k):
         out = []
@@ -124,32 +199,75 @@
             )
         return out
 
+    def name_copy(d):
+        return pltpu.make_async_remote_copy(
+            src_ref=names, dst_ref=names_got.at[g], send_sem=name_send.at[d], recv_sem=name_recv.at[d],
+            device_id=(lax.rem(g + d, n_gore), b), device_id_type=MESH,
+        )
+
+    def flag_copy(d):
+        return pltpu.make_async_remote_copy(
+            src_ref=flag, dst_ref=flag_got.at[b], send_sem=flag_send.at[d], recv_sem=flag_recv.at[d],
+            device_id=(g, lax.rem(b + d, n_band)), device_id_type=MESH,
+        )
+
+    loads[0].wait()
+    place = lax.broadcasted_iota(jnp.int32, (8, 128), 1)
+    named = jnp.zeros((8, 128), jnp.int32)
+    for r in range(CAP):
+        named = jnp.where(place == g * CAP + r, route_ref[r], named)
+    names[...] = named
+    loads[1].wait()
     for c in range(3):
         v = disp_ref[c]
         halo_g[0, c : c + 1, :] = v[0:1]
         halo_g[1, c : c + 1, :] = v[nodes_g - 1 :]
         halo_b[0, c : c + 1, :] = to_row(v[:, 0:1])
         halo_b[1, c : c + 1, :] = to_row(v[:, nodes_b - 1 :])
-    pl.semaphore_wait(barrier, n_gore + 1)
+    pl.semaphore_wait(barrier, n_gore + n_band - 2)
     first = halo_copies(0)
     for copy in first:
         copy.start()
+    for d in range(1, n_gore):
+        name_copy(d).start()
+
+    loads[3].wait()
+    loads[4].wait()
 
     def load_states(i, sums):
+        at = pl.multiple_of(i * 16, 16)
         out = []
         for c in range(3):
             pair = state_ref[c, :, pl.ds(pl.multiple_of(i * 2 * PLANE, 128), 2 * PLANE)]
             even, odd = pair[:, :PLANE], pair[:, PLANE:]
-            e_s[c, pl.ds(pl.multiple_of(i * 16, 16), 16), :] = jnp.concatenate([even, odd], axis=0)
+            e_s[c, pl.ds(at, 16), :] = jnp.concatenate([even, odd], axis=0)
             out.append(sums[c] + even + odd)
+        rows = [jnp.broadcast_to(weave_ref[pl.ds(i * 9 + t, 1), :], (CAP, 128)) for t in range(9)]
+        pair = jnp.concatenate(rows, axis=1)
+        w_s[pl.ds(at, 16), :] = jnp.concatenate([pair[:, :PLANE], pair[:, PLANE:]], axis=0)
         return tuple(out)
 
     zero = jnp.zeros((CAP, PLANE), F32)
     sums = lax.fori_loop(0, G // 2, load_states, (zero, zero, zero))
     means = [jnp.sum(s, axis=1, keepdims=True) * (1.0 / VOX) for s in sums]
 
+    for d in range(1, n_gore):
+        name_copy(d).wait()
     for copy in first:
         copy.wait()
+
+    worker = names[0:1, :]
+    for d in range(1, n_gore):
+        worker = worker + names_got[lax.rem(g + d, n_gore), 0:1, :]
+    list1, list2, list3, over = routing(worker.astype(F32), g)
+    table_v[0:1, :] = list1
+    table_v[1:2, :] = list2
+    table_v[2:3, :] = list3
+    to_scalars = pltpu.make_async_copy(table_v, table, table_sem)
+    to_scalars.start()
+    flag[...] = jnp.broadcast_to(over, (8, 128)).astype(jnp.int32)
+    for d in range(1, n_band):
+        flag_copy(d).start()
 
     inner_left, inner_right = b > 0, b < n_band - 1
     for c in range(3):
@@ -163,6 +281,7 @@
     strain_s[1] = slopes[4] + 0.5 * bz * bz
     strain_s[2] = 0.5 * (slopes[3] + slopes[1]) + 0.5 * gz * bz
 
+    loads[2].wait()
     cell_row = lax.broadcasted_iota(jnp.int32, (CAP, 1), 0)
     lane = lax.broadcasted_iota(jnp.int32, (CAP, nodes_b), 1)
     points = [yield_ref[r] for r in range(CAP)]
@@ -179,11 +298,6 @@
 
     low = lax.rem(lax.broadcasted_iota(jnp.int32, (16, PLANE), 1), G)
 
-    def stiffness_of(i):
-        even = jnp.broadcast_to(weave_ref[2 * i], (CAP, PLANE))
-        odd = jnp.broadcast_to(weave_ref[2 * i + 1], (CAP, PLANE))
-        return jnp.concatenate([even, odd], axis=0)
-
     def advance(i, sweep):
         at = pl.multiple_of(i * 16, 16)
         e = [e_s[c, pl.ds(at, 16), :] for c in range(3)]
@@ -195,7 +309,7 @@
             e[1] = e[1] + 0.5 * diff_upper(middle)
             e[2] = e[2] + 0.5 * diff_lower(middle, low)
         size = e[0] * e[0] + e[1] * e[1] + e[2] * e[2]
-        factor = stiffness_of(i) * (1.5 - 0.5 / (1.0 + size))
+        factor = w_s[pl.ds(at, 16), :] * (1.5 - 0.5 / (1.0 + size))
         return at, e, [factor * v for v in e]
 
     def parts(v):
@@ -213,6 +327,8 @@
         out = jnp.dot(both, plane_hi_ref[...], preferred_element_type=F32)
         return out[:n] + out[n:] + jnp.dot(both[:n], plane_lo_ref[...], preferred_element_type=F32)
 
+    for copy in loads[5:]:
+        copy.wait()
     for sweep in range(SWEEPS):
 
         def law(i, carry, sweep=sweep):
@@ -291,47 +407,99 @@
     slopes[4] = t1
     slopes[5] = t2
 
-    workers = [route_ref[r] for r in range(CAP)]
-
-    def slot_copy(d):
+    cells[ROWS * CAP :, :] = jnp.zeros((PACK * CAP - ROWS * CAP, 128), F32)
+    for r in range(CAP):
+
+        def gather(m, carry, r=r):
+            own[r, pl.ds(pl.multiple_of(m * 8, 8), 8), :] = cells[pl.ds(m * 64 + r, 8, stride=CAP), :]
+            return carry
+
+        lax.fori_loop(0, PACK // 8, gather, 0, unroll=True)
+    keep = pltpu.make_async_copy(own, own_ref, local_sem.at[0])
+    keep.start()
+    to_scalars.wait()
+
+    def at_index(row, position, bound):
+        return jnp.clip(table[row, position] - 1, 0, bound - 1)
+
+    def hop(semaphores, slot, source, place, ring_place, line_place, core_place):
+        send, recv = semaphores
         return pltpu.make_async_remote_copy(
-            src_ref=send.at[d],
-            dst_ref=recv_ref.at[g],
-            send_sem=send_sem.at[d],
-            recv_sem=recv_sem.at[d],
-            device_id=(lax.rem(g + d, n_gore), b),
-            device_id_type=MESH,
+            src_ref=source, dst_ref=place, send_sem=send.at[slot], recv_sem=recv.at[slot],
+            device_id=((ring_place * LINE + line_place) * CORE + core_place, b), device_id_type=MESH,
         )
 
-    def pack(d):
-        worker = lax.rem(g + d, n_gore)
-        one, two = jnp.int32(CAP), jnp.int32(CAP)
-        for r in reversed(range(CAP)):
-            named = workers[r] == worker
-            two = jnp.where(named, one, two)
-            one = jnp.where(named, r, one)
-        for k, cell in enumerate((one, two)):
-            filled = cell < CAP
-            begin = lax.rem(cell, CAP)
-
-            def rows(m, carry):
-                v = cells[pl.ds(m * 64 + begin, 8, stride=CAP), :]
-                send[d, k, pl.ds(pl.multiple_of(m * 8, 8), 8), :] = jnp.where(filled, v, 0.0)
+    one, two, three = (hop1_send, hop1_recv), (hop2_send, hop2_recv), (share_send, share_recv)
+
+    def ring_first(j):
+        to = lax.rem(y + STEPS[j], RING)
+        n = RING_FIRST
+        return hop(one, j, send1.at[pl.ds(j * n, n)], ring_got.at[pl.ds(y * n, n)], to, z, 0)
+
+    def line_first():
+        return hop(one, 0, send1.at[pl.ds(0, LINE_FIRST)], line_got, y, 1 - z, 1)
+
+    half = LINE_SECOND // 2
+
+    def line_second(j):
+        span = pl.ds(j * half, half)
+        return hop(two, j, send2.at[span], final.at[pl.ds(FINAL_RING + j * half, half)], y, 1 - z, 0)
+
+    def ring_second(j):
+        to = lax.rem(y + STEPS[j], RING)
+        n = RING_SECOND
+        return hop(two, j, send2.at[pl.ds(j * n, n)], final.at[pl.ds(FINAL_LINE + y * n, n)], to, z, 1)
+
+    def share_ring(j):
+        if j == 0:
+            return hop(three, 0, ring_got, final.at[pl.ds(0, FINAL_RING)], y, z, 1)
+        span = final.at[pl.ds(FINAL_RING + (j - 1) * half, half)]
+        return hop(three, j, span, span, y, z, 1)
+
+    def share_line(j):
+        from_y = y if j == 0 else lax.rem(y + RING - STEPS[j - 1], RING)
+        span = final.at[pl.ds(FINAL_LINE + from_y * RING_SECOND, RING_SECOND)]
+        return hop(three, j, span, span, y, z, 0)
+
+    def share_line_in(j):
+        from_y = y if j == 0 else lax.rem(y + RING - STEPS[j - 1], RING)
+        span = final.at[pl.ds(FINAL_LINE + from_y * RING_SECOND, RING_SECOND)]
+        return hop(three, j, span, span, y, z, 1)
+
+    def share_ring_in(j):
+        low, n = (0, FINAL_RING) if j == 0 else (FINAL_RING + (j - 1) * half, half)
+        span = final.at[pl.ds(low, n)]
+        return hop(three, j, span, span, y, z, 0)
+
+    @pl.when(core == 0)
+    def _():
+        for j in range(RING):
+            to = lax.rem(y + (STEPS[j] if j < 3 else 0), RING)
+
+            def fill(p, carry, j=j, to=to):
+                cell = at_index(0, to * RING_FIRST + p, CAP)
+                for m in range(PACK // 8):
+                    v = own[cell, 8 * m : 8 * m + 8, :]
+                    if j < 3:
+                        send1[j * RING_FIRST + p, 8 * m : 8 * m + 8, :] = v
+                    else:
+                        ring_got[y * RING_FIRST + p, 8 * m : 8 * m + 8, :] = v
                 return carry
 
-            lax.fori_loop(0, PACK // 8, rows, 0, unroll=True)
-
-    cells[ROWS * CAP :, :] = jnp.zeros((PACK * CAP - ROWS * CAP, 128), F32)
-
-    def dispatch(d, carry):
-        pack(d)
-        slot_copy(d).start()
-        return carry
-
-    lax.fori_loop(1, n_gore, dispatch, 0)
-    pack(0)
-    own = pltpu.make_async_copy(send.at[0], recv_ref.at[g], own_sem)
-    own.start()
+            lax.fori_loop(0, RING_FIRST, fill, 0)
+            if j < 3:
+                ring_first(j).start()
+
+    @pl.when(core == 1)
+    def _():
+        def fill(p, carry):
+            cell = at_index(0, p, CAP)
+            for m in range(PACK // 8):
+                send1[p, 8 * m : 8 * m + 8, :] = own[cell, 8 * m : 8 * m + 8, :]
+            return carry
+
+        lax.fori_loop(0, LINE_FIRST, fill, 0)
+        line_first().start()
 
     for copy in second:
         copy.wait()
@@ -347,16 +515,86 @@
         if c == 2:
             value = value + press_ref[...]
         force_ref[c] = value
-
-    own.wait()
-
-    def settle(d, carry):
-        copy = slot_copy(d)
-        copy.wait_send()
-        copy.wait_recv()
-        return carry
-
-    lax.fori_loop(1, n_gore, settle, 0)
+    for d in range(1, n_band):
+        flag_copy(d).wait()
+    total = flag[...]
+    for d in range(1, n_band):
+        total = total + flag_got[lax.rem(b + d, n_band)]
+    flag_ref[...] = total
+
+    @pl.when(core == 0)
+    def _():
+        for j in range(3):
+            ring_first(j).wait()
+        for j in range(2):
+
+            def fill(p, carry):
+                cell = at_index(1, p, FINAL_RING)
+                for m in range(PACK // 8):
+                    send2[p, 8 * m : 8 * m + 8, :] = ring_got[cell, 8 * m : 8 * m + 8, :]
+                return carry
+
+            lax.fori_loop(j * half, (j + 1) * half, fill, 0)
+            line_second(j).start()
+        share_ring(0).start()
+        stay = pltpu.make_async_copy(ring_got, final.at[pl.ds(0, FINAL_RING)], local_sem.at[1])
+        stay.start()
+        for j in range(2):
+            line_second(j).wait()
+            share_ring(1 + j).start()
+        stay.wait()
+        for j in range(3):
+            share_ring(j).wait_send()
+        for j in range(4):
+            share_line_in(j).wait_recv()
+
+    @pl.when(core == 1)
+    def _():
+        line_first().wait()
+        for j in range(4):
+            to = lax.rem(y + (STEPS[j] if j < 3 else 0), RING)
+
+            def fill(p, carry, j=j, to=to):
+                index = at_index(1, to * RING_SECOND + p, 2 * CAP)
+                mine = index < CAP
+                here, there = jnp.minimum(index, CAP - 1), jnp.maximum(index - CAP, 0)
+                for m in range(PACK // 8):
+                    v = jnp.where(mine, own[here, 8 * m : 8 * m + 8, :], line_got[there, 8 * m : 8 * m + 8, :])
+                    if j < 3:
+                        send2[j * RING_SECOND + p, 8 * m : 8 * m + 8, :] = v
+                    else:
+                        final[FINAL_LINE + y * RING_SECOND + p, 8 * m : 8 * m + 8, :] = v
+                return carry
+
+            lax.fori_loop(0, RING_SECOND, fill, 0)
+            if j < 3:
+                ring_second(j).start()
+        share_line(0).start()
+        for j in range(3):
+            ring_second(j).wait()
+            share_line(1 + j).start()
+        for j in range(4):
+            share_line(j).wait_send()
+        for j in range(3):
+            share_ring_in(j).wait_recv()
+
+    stores = []
+    for t in range(GROUP * MOST // 8):
+
+        def choose(p, carry):
+            filled = table[2, p] > 0
+            cell = at_index(2, p, FINAL)
+            for m in range(PACK // 8):
+                chosen[p, 8 * m : 8 * m + 8, :] = jnp.where(filled, final[cell, 8 * m : 8 * m + 8, :], 0.0)
+            return carry
+
+        lax.fori_loop(8 * t, 8 * t + 8, choose, 0)
+        span = pl.ds(8 * t, 8)
+        stores.append(pltpu.make_async_copy(chosen.at[span], result_ref.at[span], out_sem.at[t]))
+        stores[-1].start()
+    keep.wait()
+    for copy in stores:
+        copy.wait()
 
 
 def layout_kernel(slots, recv_ref, out_ref, got, made, in_sem, out_sem):
@@ -389,64 +627,9 @@
         copy.wait()
 
 
-def local(displacement, stiffness, pressure, yield_points, route, cell_state, weave):
-    n_gore, n_band = lax.axis_size("gore"), lax.axis_size("band")
-    slots = n_gore * MOST
-    nodes_g, nodes_b = stiffness.shape
-    plane_high, plane_low, line, weight = tables()
-    vmem, smem = pl.BlockSpec(memory_space=pltpu.VMEM), pl.BlockSpec(memory_space=pltpu.SMEM)
-    any_space = pl.BlockSpec(memory_space=pl.ANY)
-    n = G * CAP
-
-    def run(*args):
-        return pl.pallas_call(
-            lambda *refs: kernel(n_gore, n_band, *refs),
-            out_shape=(
-                jax.ShapeDtypeStruct((3, nodes_g, nodes_b), F32),
-                jax.ShapeDtypeStruct((n_gore, MOST, PACK, 128), F32),
-            ),
-            in_specs=[smem, smem] + [vmem] * 9,
-            out_specs=(vmem, any_space),
-            scratch_shapes=[
-                pltpu.VMEM((4, 8, nodes_b), F32),
-                pltpu.VMEM((4, 8, nodes_g), F32),
-                pltpu.VMEM((4, 8, nodes_b), F32),
-                pltpu.VMEM((4, 8, nodes_g), F32),
-                pltpu.VMEM((6, nodes_g, nodes_b), F32),
-                pltpu.VMEM((3, nodes_g, nodes_b), F32),
-                pltpu.VMEM((3, n, PLANE), F32),
-                pltpu.VMEM((n + 16, PLANE), F32),
-                pltpu.VMEM((n, PLANE), F32),
-                pltpu.VMEM((2 * n, PLANE), BF16),
-                pltpu.VMEM((n + 16, PLANE), F32),
-                pltpu.VMEM((PACK * CAP, 128), F32),
-                pltpu.VMEM((n_gore, MOST, PACK, 128), F32),
-                pltpu.SemaphoreType.DMA((8,)),
-                pltpu.SemaphoreType.DMA((8,)),
-                pltpu.SemaphoreType.DMA((n_gore,)),
-                pltpu.SemaphoreType.DMA((n_gore,)),
-                pltpu.SemaphoreType.DMA,
-            ],
-            compiler_params=pltpu.CompilerParams(
-                collective_id=0, has_side_effects=True, vmem_limit_bytes=48 * 2**20
-            ),
-            name="cells",
-        )(*args)
-
-    force, recv = run(
-        yield_points,
-        route.reshape(-1),
-        displacement,
-        stiffness,
-        pressure,
-        cell_state.transpose(1, 0, 2),
-        weave.reshape(G, 1, PLANE),
-        jnp.asarray(plane_high),
-        jnp.asarray(plane_low),
-        jnp.asarray(line),
-        jnp.asarray(weight),
-    )
-    cell_strain = pl.pallas_call(
+def fast_layout(slots, result):
+    any_space = pl.BlockSpec(memory_space=pltpu.HBM)
+    return pl.pallas_call(
         lambda *refs: layout_kernel(slots, *refs),
         out_shape=jax.ShapeDtypeStruct((3, slots, VOX), F32),
         in_specs=[any_space],
@@ -459,7 +642,118 @@
         ],
         compiler_params=pltpu.CompilerParams(vmem_limit_bytes=32 * 2**20),
         name="layout",
-    )(recv.reshape(slots, PACK, 128))
+    )(result)
+
+
+def send_all(workers, own, n_gore, slots):
+    states = own[:, :ROWS].reshape(CAP, 3, VOX)
+    onehot = (workers[:, None] == jnp.arange(n_gore, dtype=jnp.int32)[None, :]).astype(jnp.int32)
+    earlier = jnp.cumsum(onehot, axis=0) - onehot
+    slot_index = workers * MOST + jnp.sum(earlier * onehot, axis=1)
+    outgoing = jnp.zeros((slots, 3, VOX), F32).at[slot_index].set(states)
+    arrived = lax.all_to_all(
+        outgoing.reshape(n_gore, MOST, 3, VOX), "gore", split_axis=0, concat_axis=0, tiled=True
+    )
+    return arrived.reshape(slots, 3, VOX).transpose(1, 0, 2)
+
+
+def local(displacement, stiffness, pressure, yield_points, route, cell_state, weave):
+    n_gore, n_band = lax.axis_size("gore"), lax.axis_size("band")
+    slots = n_gore * MOST
+    nodes_g, nodes_b = stiffness.shape
+    plane_high, plane_low, line, weight = tables()
+    vmem, hbm = pl.BlockSpec(memory_space=pltpu.VMEM), pl.BlockSpec(memory_space=pltpu.HBM)
+    n = G * CAP
+    vm, dma = pltpu.VMEM, pltpu.SemaphoreType.DMA
+    workers = route.reshape(-1)
+    force, flag, result, own = pl.pallas_call(
+        lambda *refs: kernel(n_gore, n_band, *refs),
+        out_shape=(
+            jax.ShapeDtypeStruct((3, nodes_g, nodes_b), F32),
+            jax.ShapeDtypeStruct((8, 128), jnp.int32),
+            jax.ShapeDtypeStruct((slots, PACK, 128), F32),
+            jax.ShapeDtypeStruct((CAP, PACK, 128), F32),
+        ),
+        in_specs=[hbm] * 11,
+        out_specs=(vmem, vmem, hbm, hbm),
+        scratch_shapes=[
+            pltpu.SMEM((CAP,), jnp.int32),
+            pltpu.SMEM((CAP,), jnp.int32),
+            vm((3, nodes_g, nodes_b), F32),
+            vm((nodes_g, nodes_b), F32),
+            vm((nodes_g, nodes_b), F32),
+            vm((3, CAP, VOX), F32),
+            vm((VOX // 128, 128), F32),
+            vm((PLANE, PLANE), BF16),
+            vm((PLANE, PLANE), BF16),
+            vm((2 * n, n), BF16),
+            vm((G, 1, PLANE), F32),
+            vm((4, 8, nodes_b), F32),
+            vm((4, 8, nodes_g), F32),
+            vm((4, 8, nodes_b), F32),
+            vm((4, 8, nodes_g), F32),
+            vm((6, nodes_g, nodes_b), F32),
+            vm((3, nodes_g, nodes_b), F32),
+            vm((3, n, PLANE), F32),
+            vm((n, PLANE), F32),
+            vm((n + 16, PLANE), F32),
+            vm((n, PLANE), F32),
+            vm((2 * n, PLANE), BF16),
+            vm((n + 16, PLANE), F32),
+            vm((PACK * CAP, 128), F32),
+            vm((8, 128), jnp.int32),
+            vm((n_gore, 8, 128), jnp.int32),
+            vm((8, 128), jnp.int32),
+            vm((n_band, 8, 128), jnp.int32),
+            vm((8, 128), jnp.int32),
+            pltpu.SMEM((8, 128), jnp.int32),
+            vm((CAP, PACK, 128), F32),
+            vm((3 * RING_FIRST, PACK, 128), F32),
+            vm((3 * RING_SECOND, PACK, 128), F32),
+            vm((FINAL_RING, PACK, 128), F32),
+            vm((LINE_FIRST, PACK, 128), F32),
+            vm((FINAL, PACK, 128), F32),
+            vm((slots, PACK, 128), F32),
+            dma((11,)),
+            dma((8,)),
+            dma((8,)),
+            dma((n_gore,)),
+            dma((n_gore,)),
+            dma((n_band,)),
+            dma((n_band,)),
+            dma,
+            dma((3,)),
+            dma((3,)),
+            dma((3,)),
+            dma((3,)),
+            dma((4,)),
+            dma((4,)),
+            dma((2,)),
+            dma((slots // 8,)),
+        ],
+        compiler_params=pltpu.CompilerParams(
+            collective_id=0, has_side_effects=True, vmem_limit_bytes=56 * 2**20
+        ),
+        name="cells",
+    )(
+        yield_points,
+        workers,
+        displacement,
+        stiffness,
+        pressure,
+        cell_state.transpose(1, 0, 2),
+        weave.reshape(VOX // 128, 128),
+        jnp.asarray(plane_high),
+        jnp.asarray(plane_low),
+        jnp.asarray(line),
+        jnp.asarray(weight),
+    )
+    cell_strain = lax.cond(
+        flag[0, 0] == 0,
+        lambda result, own, workers: fast_layout(slots, result),
+        lambda result, own, workers: send_all(workers, own, n_gore, slots),
+        result, own, workers,
+    )
     return force, cell_strain.transpose(1, 0, 2)
 
 

time: 138 us -> 175 us (1.27)
  the two profiles are of different devices: /device:TPU:49 before, /device:TPU:1 now
where the time goes in v2:
time: 175 us
  Pallas kernels  79 us (45%)
  blocking collectives  65.4 us (37%)
  local copies, waits for them, and re-layouts  26.9 us (15%)
  other arithmetic  2.3 us (1%)
    pallas_call x1, Pallas kernels, local(): pl.pallas_call(lambda *refs: kernel(n_gore, n_band, *refs), out_shape=(ja...  79 us
    all_to_all x1, blocking collectives, send_all(): lax.all_to_all(outgoing.reshape(n_gore, MOST, 3, VOX), 'gore', split_axis...  65.4 us
    reshape x1, local copies, waits for them, and re-layouts, send_all(): return arrived.reshape(slots, 3, VOX).transpose(1, 0, 2)  7.04 us
    reshape x1, local copies, waits for them, and re-layouts, send_all(): outgoing.reshape(n_gore, MOST, 3, VOX)  5.74 us
    scatter x1, local copies, waits for them, and re-layouts, send_all(): outgoing = jnp.zeros((slots, 3, VOX), F32).at[slot_index].set(states)  5.04 us
    another operation x1, local copies, waits for them, and re-layouts  3.82 us

profile of v2, /device:TPU:1, one launch (start us, length us, event | category | flops | bytes accessed | tf_op | source)
XLA Modules:
  0.0 175.0 jit_solution(2610839021199747658)
XLA Ops:
  0.6 79.0 %cells.1 = (f32[3,128,256]{2,1,0:T(8,128)}, s32[8,128]{1,0:T(8,128)}, f32[32,328,128]{2,1,0:T(8,128)}, f32[8,328,128]{2,1,0:T(8,128)S(1)}) custom-call(s32[8]{0:T(128)} %refs_0_.2, s32[8]{0:T(128)} %bitcast.18, f32[3,128,256]{2,1,0:T(8,128)} %refs_2_.1, f32[128,256]{1,0:T(8,128)} %refs_3_.1, f32[128,256]{1,0:T(8,128)} %refs_4_.1, f32[3,8,13824]{2,1,0:T(8,128)} %bitcast.16, ...), custom_call_target="tpu_custom_call" | custom-call | tf_op jit(solution)/shard_map/cells/pallas_call | solution.py:669
  79.7 1.2 slice.6
  81.5 0.0 copy-start
  81.5 92.7 %conditional.1 = (f32[3,32,13824]{2,1,0:T(8,128)}) conditional(s32[]{:T(128)} %bitcast.6, (s32[8]{0:T(128)}, s32[8,1]{0,1:T(1,128)}, f32[8,328,128]{2,1,0:T(8,128)S(1)}) %tuple.20, f32[32,328,128]{2,1,0:T(8,128)} %get-tuple-element.22), branch_computations={%region_0.4_spmd, %region_4.5_spmd} | conditional | flops 1824 | bytes 54413552 | solution.py:751
  81.6 0.8 fusion
  82.4 0.8 select_reduce_fusion
  83.2 0.7 reshape.30
  83.9 0.7 compare_select_fusion
  84.5 3.8 %broadcast.10 = f32[32,3,13824]{2,1,0:T(4,128)} broadcast(f32[]{:T(128)} %constant.9.clone), dimensions={} | broadcast | bytes 5308420 | tf_op jit(solution)/shard_map/broadcast.4
  88.3 5.0 %scatter_fusion = f32[32,3,13824]{2,1,0:T(4,128)} fusion(f32[32,3,13824]{2,1,0:T(4,128)} %broadcast.10, s32[8]{0:T(128)S(1)} %compare_select_fusion, f32[8,3,13824]{2,1,0:T(4,128)S(1)} %reshape.30), kind=kCustom, calls=%fused_computation | custom fusion | bytes 3981344 | tf_op jit(solution)/shard_map/cond/branch_0_fun/scatter | solution.py:653
  93.4 5.7 %copy.25 = f32[16,2,3,13824]{3,1,2,0:T(2,128)S(1)} copy(f32[16,2,3,13824]{3,2,1,0:T(4,128)} %bitcast.12) | data formatting | bytes 10616832 | tf_op jit(solution)/shard_map/cond/branch_0_fun/reshape | solution.py:655
  99.1 65.4 %all_to_all.4 = f32[16,2,3,13824]{3,1,2,0:T(2,128)S(1)} all-to-all(f32[16,2,3,13824]{3,1,2,0:T(2,128)S(1)} %copy.25), channel_id=1, replica_groups=mesh['gore'=16,'band'=8] {'gore'}, dimensions={0} | all-to-all | bytes 10616832 | tf_op jit(solution)/shard_map/cond/branch_0_fun/all_to_all | solution.py:654
  164.6 2.7 %copy.26 = f32[16,2,3,13824]{3,1,0,2:T(2,128)} copy(f32[16,2,3,13824]{3,1,2,0:T(2,128)S(1)} %all_to_all.4) | data formatting | bytes 10616832 | tf_op jit(solution)/shard_map/cond/branch_0_fun/all_to_all | solution.py:654
  167.2 7.0 %reshape.20 = f32[32,3,13824]{2,0,1:T(8,128)} reshape(f32[16,2,3,13824]{3,1,0,2:T(2,128)} %copy.26) | data formatting | bytes 10616832 | tf_op jit(solution)/shard_map/cond/branch_0_fun/reshape | solution.py:657
  174.3 0.0 copy-done
  174.3 0.7 copy.33
  (1 shorter events, 0.0 us)
Async XLA Ops:
  81.5 92.7 %copy-start = (f32[3,128,256]{2,1,0:T(8,128)S(1)}, f32[3,128,256]{2,1,0:T(8,128)}, u32[]{:S(2)}) copy-start(f32[3,128,256]{2,1,0:T(8,128)} %get-tuple-element.25) | copy-start | bytes 1179652

commit v3 on v2

--- a/solution.py
+++ b/solution.py
@@ -115,52 +115,54 @@
         key = key.astype(F32)
         return rank_of(key, to_column(key), earlier).astype(jnp.int32)
 
-    ring_first = rank(source * RING + to_y)
-    line_second = rank(jnp.where(first & crossing, from_z * RING + to_y, alone))
-    line_first = rank(jnp.where(crossing, source, alone))
-    ring_second = rank(jnp.where(first, alone, (from_y * RING + to_y) * LINE + to_z))
-    slot = rank(source * GROUP + to)
-    over = first & ((ring_first >= RING_FIRST) | (crossing & (line_second >= LINE_SECOND)))
-    over = over | (jnp.logical_not(first) & (ring_second >= RING_SECOND))
-
     own, mine = source == g, from_c == c
     at_ring = c == 0
     cell = lane & 7
-    place1_ring = jnp.where(own, to_y * RING_FIRST + ring_first, -1)
-    place1 = jnp.where(at_ring, place1_ring, jnp.where(own & crossing, line_first, -1))
-    place2_ring = jnp.where(mine & crossing & (from_z == z) & (to_y == y), line_second, -1)
-    place2_line = jnp.where(mine & (from_y == y) & (to_z == z), to_y * RING_SECOND + ring_second, -1)
-    place2 = jnp.where(at_ring, place2_ring, place2_line)
-    from_ring = from_y * RING_FIRST + ring_first
-    from_line = jnp.where(from_z == z, cell, CAP + line_first)
-    index2 = jnp.where(at_ring, from_ring, from_line)
-    place3 = jnp.where(to == g, source * MOST + slot, -1)
-    index3 = jnp.where(crossing, FINAL_RING + line_second, from_ring)
-    index3 = jnp.where(first, index3, FINAL_LINE + from_y * RING_SECOND + ring_second)
-
     column = lax.broadcasted_iota(jnp.int32, (n, n), 1).astype(F32)
 
     def listing(place, index):
         place, index = to_column(place.astype(F32)), to_column(index.astype(F32) + 1.0)
         return jnp.sum(jnp.where(place == column, index, 0.0), axis=0, keepdims=True).astype(jnp.int32)
 
-    over = jnp.sum(jnp.where(over, 1.0, 0.0), axis=1, keepdims=True)
-    return listing(place1, cell), listing(place2, index2), listing(place3, index3), over
+    ring_first = rank(source * RING + to_y)
+    line_first = rank(jnp.where(crossing, source, alone))
+    place1_ring = jnp.where(own, to_y * RING_FIRST + ring_first, -1)
+    place1 = jnp.where(at_ring, place1_ring, jnp.where(own & crossing, line_first, -1))
+
+    def later():
+        line_second = rank(jnp.where(first & crossing, from_z * RING + to_y, alone))
+        ring_second = rank(jnp.where(first, alone, (from_y * RING + to_y) * LINE + to_z))
+        slot = rank(source * GROUP + to)
+        over = first & ((ring_first >= RING_FIRST) | (crossing & (line_second >= LINE_SECOND)))
+        over = over | (jnp.logical_not(first) & (ring_second >= RING_SECOND))
+        place2_ring = jnp.where(mine & crossing & (from_z == z) & (to_y == y), line_second, -1)
+        place2_line = jnp.where(mine & (from_y == y) & (to_z == z), to_y * RING_SECOND + ring_second, -1)
+        place2 = jnp.where(at_ring, place2_ring, place2_line)
+        from_ring = from_y * RING_FIRST + ring_first
+        from_line = jnp.where(from_z == z, cell, CAP + line_first)
+        index2 = jnp.where(at_ring, from_ring, from_line)
+        place3 = jnp.where(to == g, source * MOST + slot, -1)
+        index3 = jnp.where(crossing, FINAL_RING + line_second, from_ring)
+        index3 = jnp.where(first, index3, FINAL_LINE + from_y * RING_SECOND + ring_second)
+        over = jnp.sum(jnp.where(over, 1.0, 0.0), axis=1, keepdims=True)
+        return listing(place2, index2), listing(place3, index3), over
+
+    return listing(place1, cell), later
 
 
 def kernel(
     n_gore, n_band,
     yield_hbm, route_hbm, disp_hbm, stiff_hbm, press_hbm, state_hbm, weave_hbm,
     plane_hi_hbm, plane_lo_hbm, line_hbm, weight_hbm,
-    force_ref, flag_ref, result_ref, own_ref,
+    force_ref, flag_ref, table_ref, final, own_ref,
     yield_ref, route_ref, disp_ref, stiff_ref, press_ref, state_ref, weave_ref,
     plane_hi_ref, plane_lo_ref, line_ref, weight_ref,
     halo_g, halo_b, got_g, got_b, slopes, strain_s,
     e_s, w_s, s_pad, d_s, x_s, f_s, cells,
-    names, names_got, flag, flag_got, table_v, table,
-    own, send1, send2, ring_got, line_got, final, chosen,
+    names, names_got, flag, flag_got, hop1_v, hop1_table, table_v, table,
+    own, send1, send2, ring_got, line_got, here_got,
     in_sem, halo_send, halo_recv, name_send, name_recv, flag_send, flag_recv, table_sem,
-    hop1_send, hop1_recv, hop2_send, hop2_recv, share_send, share_recv, local_sem, out_sem,
+    hop1_send, hop1_recv, hop2_send, hop2_recv, share_send, share_recv, local_sem,
 ):
     g, b = lax.axis_index("gore"), lax.axis_index("band")
     y, z, core = lax.div(g, LINE * CORE), lax.rem(lax.div(g, CORE), LINE), lax.rem(g, CORE)
@@ -248,7 +250,7 @@
         return tuple(out)
 
     zero = jnp.zeros((CAP, PLANE), F32)
-    sums = lax.fori_loop(0, G // 2, load_states, (zero, zero, zero))
+    sums = lax.fori_loop(0, G // 2, load_states, (zero, zero, zero), unroll=2)
     means = [jnp.sum(s, axis=1, keepdims=True) * (1.0 / VOX) for s in sums]
 
     for d in range(1, n_gore):
@@ -259,15 +261,9 @@
     worker = names[0:1, :]
     for d in range(1, n_gore):
         worker = worker + names_got[lax.rem(g + d, n_gore), 0:1, :]
-    list1, list2, list3, over = routing(worker.astype(F32), g)
-    table_v[0:1, :] = list1
-    table_v[1:2, :] = list2
-    table_v[2:3, :] = list3
-    to_scalars = pltpu.make_async_copy(table_v, table, table_sem)
-    to_scalars.start()
-    flag[...] = jnp.broadcast_to(over, (8, 128)).astype(jnp.int32)
-    for d in range(1, n_band):
-        flag_copy(d).start()
+    hop1_v[...] = jnp.broadcast_to(routing(worker.astype(F32), g)[0], (8, 128))
+    hop1_scalars = pltpu.make_async_copy(hop1_v, hop1_table, table_sem.at[0])
+    hop1_scalars.start()
 
     inner_left, inner_right = b > 0, b < n_band - 1
     for c in range(3):
@@ -339,7 +335,7 @@
             d_s[pl.ds(at, 16), :] = diff_upper(s[1]) + diff_lower(s[2], low)
             return carry
 
-        lax.fori_loop(0, G // 2, law, 0)
+        lax.fori_loop(0, G // 2, law, 0, unroll=6)
         s_pad[0:8, :] = s_pad[G * 8 : G * 8 + 8, :]
         s_pad[G * 8 + 8 :, :] = s_pad[8:16, :]
 
@@ -351,7 +347,7 @@
             x_s[pl.ds(G * CAP + at, 16), :] = rest
             return carry
 
-        lax.fori_loop(0, G // 2, source, 0)
+        lax.fori_loop(0, G // 2, source, 0, unroll=6)
         spectrum = lines(planes(x_s[...]))
         weight = jnp.broadcast_to(weight_ref[...], (G, CAP, PLANE)).reshape(G * CAP, PLANE)
         back = lines(spectrum * weight)
@@ -373,8 +369,116 @@
             out.append(sums[c] + s[c][0:8] + s[c][8:16])
         return tuple(out)
 
-    sums = lax.fori_loop(0, G // 2, finish, (zero, zero, zero))
+    sums = lax.fori_loop(0, G // 2, finish, (zero, zero, zero), unroll=2)
     point_stress = [jnp.sum(s, axis=1, keepdims=True) * (1.0 / VOX) for s in sums]
+
+    cells[ROWS * CAP :, :] = jnp.zeros((PACK * CAP - ROWS * CAP, 128), F32)
+    hop1_scalars.wait()
+
+    def at_index(table, row, position, bound):
+        return jnp.clip(table[row, position] - 1, 0, bound - 1)
+
+    def tiles_of(cell, m):
+        return cells[pl.ds(m * 64 + cell, 8, stride=CAP), :]
+
+    def hop(semaphores, slot, source, place, ring_place, line_place, core_place):
+        send, recv = semaphores
+        return pltpu.make_async_remote_copy(
+            src_ref=source, dst_ref=place, send_sem=send.at[slot], recv_sem=recv.at[slot],
+            device_id=((ring_place * LINE + line_place) * CORE + core_place, b), device_id_type=MESH,
+        )
+
+    one, two, three = (hop1_send, hop1_recv), (hop2_send, hop2_recv), (share_send, share_recv)
+
+    def ring_first(j):
+        to = lax.rem(y + STEPS[j], RING)
+        n = RING_FIRST
+        return hop(one, j, send1.at[pl.ds(j * n, n)], ring_got.at[pl.ds(y * n, n)], to, z, 0)
+
+    def line_first():
+        return hop(one, 0, send1.at[pl.ds(0, LINE_FIRST)], line_got, y, 1 - z, 1)
+
+    half = LINE_SECOND // 2
+
+    def line_second(j):
+        span = pl.ds(j * half, half)
+        return hop(two, j, send2.at[span], final.at[pl.ds(FINAL_RING + j * half, half)], y, 1 - z, 0)
+
+    def ring_second(j):
+        to = lax.rem(y + STEPS[j], RING)
+        n = RING_SECOND
+        return hop(two, j, send2.at[pl.ds(j * n, n)], final.at[pl.ds(FINAL_LINE + y * n, n)], to, z, 1)
+
+    def share_ring(j):
+        if j == 0:
+            return hop(three, 0, ring_got, final.at[pl.ds(0, FINAL_RING)], y, z, 1)
+        span = final.at[pl.ds(FINAL_RING + (j - 1) * half, half)]
+        return hop(three, j, span, span, y, z, 1)
+
+    def share_line(j):
+        from_y = y if j == 0 else lax.rem(y + RING - STEPS[j - 1], RING)
+        span = final.at[pl.ds(FINAL_LINE + from_y * RING_SECOND, RING_SECOND)]
+        return hop(three, j, here_got if j == 0 else span, span, y, z, 0)
+
+    def share_line_in(j):
+        from_y = y if j == 0 else lax.rem(y + RING - STEPS[j - 1], RING)
+        span = final.at[pl.ds(FINAL_LINE + from_y * RING_SECOND, RING_SECOND)]
+        return hop(three, j, span, span, y, z, 1)
+
+    def share_ring_in(j):
+        low, n = (0, FINAL_RING) if j == 0 else (FINAL_RING + (j - 1) * half, half)
+        span = final.at[pl.ds(low, n)]
+        return hop(three, j, span, span, y, z, 0)
+
+    @pl.when(core == 0)
+    def _():
+        for j in range(RING):
+            to = lax.rem(y + (STEPS[j] if j < 3 else 0), RING)
+
+            def fill(p, carry, j=j, to=to):
+                cell = at_index(hop1_table, 0, to * RING_FIRST + p, CAP)
+                for m in range(PACK // 8):
+                    v = tiles_of(cell, m)
+                    if j < 3:
+                        send1[j * RING_FIRST + p, 8 * m : 8 * m + 8, :] = v
+                    else:
+                        ring_got[y * RING_FIRST + p, 8 * m : 8 * m + 8, :] = v
+                return carry
+
+            lax.fori_loop(0, RING_FIRST, fill, 0)
+            if j < 3:
+                ring_first(j).start()
+
+    @pl.when(core == 1)
+    def _():
+        def fill(p, carry):
+            cell = at_index(hop1_table, 0, p, CAP)
+            for m in range(PACK // 8):
+                send1[p, 8 * m : 8 * m + 8, :] = tiles_of(cell, m)
+            return carry
+
+        lax.fori_loop(0, LINE_FIRST, fill, 0)
+        line_first().start()
+
+    list2, list3, over = routing(worker.astype(F32), g)[1]()
+    table_v[0:1, :] = list2
+    table_v[1:2, :] = list3
+    to_scalars = pltpu.make_async_copy(table_v, table, table_sem.at[1])
+    to_scalars.start()
+    hand_on = pltpu.make_async_copy(table_v, table_ref, table_sem.at[2])
+    hand_on.start()
+    flag[...] = jnp.broadcast_to(over, (8, 128)).astype(jnp.int32)
+    for d in range(1, n_band):
+        flag_copy(d).start()
+    for r in range(CAP):
+
+        def gather(m, carry, r=r):
+            own[r, pl.ds(pl.multiple_of(m * 8, 8), 8), :] = cells[pl.ds(m * 64 + r, 8, stride=CAP), :]
+            return carry
+
+        lax.fori_loop(0, PACK // 8, gather, 0, unroll=True)
+    keep = pltpu.make_async_copy(own, own_ref, local_sem.at[0])
+    keep.start()
 
     stiff = stiff_ref[...]
     e11, e22, e12 = strain_s[0], strain_s[1], strain_s[2]
@@ -407,99 +511,55 @@
     slopes[4] = t1
     slopes[5] = t2
 
-    cells[ROWS * CAP :, :] = jnp.zeros((PACK * CAP - ROWS * CAP, 128), F32)
-    for r in range(CAP):
-
-        def gather(m, carry, r=r):
-            own[r, pl.ds(pl.multiple_of(m * 8, 8), 8), :] = cells[pl.ds(m * 64 + r, 8, stride=CAP), :]
-            return carry
-
-        lax.fori_loop(0, PACK // 8, gather, 0, unroll=True)
-    keep = pltpu.make_async_copy(own, own_ref, local_sem.at[0])
-    keep.start()
     to_scalars.wait()
 
-    def at_index(row, position, bound):
-        return jnp.clip(table[row, position] - 1, 0, bound - 1)
-
-    def hop(semaphores, slot, source, place, ring_place, line_place, core_place):
-        send, recv = semaphores
-        return pltpu.make_async_remote_copy(
-            src_ref=source, dst_ref=place, send_sem=send.at[slot], recv_sem=recv.at[slot],
-            device_id=((ring_place * LINE + line_place) * CORE + core_place, b), device_id_type=MESH,
-        )
-
-    one, two, three = (hop1_send, hop1_recv), (hop2_send, hop2_recv), (share_send, share_recv)
-
-    def ring_first(j):
-        to = lax.rem(y + STEPS[j], RING)
-        n = RING_FIRST
-        return hop(one, j, send1.at[pl.ds(j * n, n)], ring_got.at[pl.ds(y * n, n)], to, z, 0)
-
-    def line_first():
-        return hop(one, 0, send1.at[pl.ds(0, LINE_FIRST)], line_got, y, 1 - z, 1)
-
-    half = LINE_SECOND // 2
-
-    def line_second(j):
-        span = pl.ds(j * half, half)
-        return hop(two, j, send2.at[span], final.at[pl.ds(FINAL_RING + j * half, half)], y, 1 - z, 0)
-
-    def ring_second(j):
-        to = lax.rem(y + STEPS[j], RING)
-        n = RING_SECOND
-        return hop(two, j, send2.at[pl.ds(j * n, n)], final.at[pl.ds(FINAL_LINE + y * n, n)], to, z, 1)
-
-    def share_ring(j):
-        if j == 0:
-            return hop(three, 0, ring_got, final.at[pl.ds(0, FINAL_RING)], y, z, 1)
-        span = final.at[pl.ds(FINAL_RING + (j - 1) * half, half)]
-        return hop(three, j, span, span, y, z, 1)
-
-    def share_line(j):
-        from_y = y if j == 0 else lax.rem(y + RING - STEPS[j - 1], RING)
-        span = final.at[pl.ds(FINAL_LINE + from_y * RING_SECOND, RING_SECOND)]
-        return hop(three, j, span, span, y, z, 0)
-
-    def share_line_in(j):
-        from_y = y if j == 0 else lax.rem(y + RING - STEPS[j - 1], RING)
-        span = final.at[pl.ds(FINAL_LINE + from_y * RING_SECOND, RING_SECOND)]
-        return hop(three, j, span, span, y, z, 1)
-
-    def share_ring_in(j):
-        low, n = (0, FINAL_RING) if j == 0 else (FINAL_RING + (j - 1) * half, half)
-        span = final.at[pl.ds(low, n)]
-        return hop(three, j, span, span, y, z, 0)
+    def stay_here():
+        span = pl.ds(FINAL_LINE + y * RING_SECOND, RING_SECOND)
+        return pltpu.make_async_copy(here_got, final.at[span], local_sem.at[1])
+
+    def stay():
+        return pltpu.make_async_copy(ring_got, final.at[pl.ds(0, FINAL_RING)], local_sem.at[1])
 
     @pl.when(core == 0)
     def _():
-        for j in range(RING):
-            to = lax.rem(y + (STEPS[j] if j < 3 else 0), RING)
-
-            def fill(p, carry, j=j, to=to):
-                cell = at_index(0, to * RING_FIRST + p, CAP)
+        for j in range(3):
+            ring_first(j).wait()
+        for j in range(2):
+
+            def fill(p, carry):
+                cell = at_index(table, 0, p, FINAL_RING)
                 for m in range(PACK // 8):
-                    v = own[cell, 8 * m : 8 * m + 8, :]
-                    if j < 3:
-                        send1[j * RING_FIRST + p, 8 * m : 8 * m + 8, :] = v
-                    else:
-                        ring_got[y * RING_FIRST + p, 8 * m : 8 * m + 8, :] = v
+                    send2[p, 8 * m : 8 * m + 8, :] = ring_got[cell, 8 * m : 8 * m + 8, :]
                 return carry
 
-            lax.fori_loop(0, RING_FIRST, fill, 0)
-            if j < 3:
-                ring_first(j).start()
+            lax.fori_loop(j * half, (j + 1) * half, fill, 0)
+            line_second(j).start()
+        share_ring(0).start()
+        stay().start()
 
     @pl.when(core == 1)
     def _():
-        def fill(p, carry):
-            cell = at_index(0, p, CAP)
-            for m in range(PACK // 8):
-                send1[p, 8 * m : 8 * m + 8, :] = own[cell, 8 * m : 8 * m + 8, :]
-            return carry
-
-        lax.fori_loop(0, LINE_FIRST, fill, 0)
-        line_first().start()
+        line_first().wait()
+        for j in range(4):
+            to = lax.rem(y + (STEPS[j] if j < 3 else 0), RING)
+
+            def fill(p, carry, j=j, to=to):
+                index = at_index(table, 0, to * RING_SECOND + p, 2 * CAP)
+                mine = index < CAP
+                here, there = jnp.minimum(index, CAP - 1), jnp.maximum(index - CAP, 0)
+                for m in range(PACK // 8):
+                    v = jnp.where(mine, own[here, 8 * m : 8 * m + 8, :], line_got[there, 8 * m : 8 * m + 8, :])
+                    if j < 3:
+                        send2[j * RING_SECOND + p, 8 * m : 8 * m + 8, :] = v
+                    else:
+                        here_got[p, 8 * m : 8 * m + 8, :] = v
+                return carry
+
+            lax.fori_loop(0, RING_SECOND, fill, 0)
+            if j < 3:
+                ring_second(j).start()
+        share_line(0).start()
+        stay_here().start()
 
     for copy in second:
         copy.wait()
@@ -515,134 +575,108 @@
         if c == 2:
             value = value + press_ref[...]
         force_ref[c] = value
+    @pl.when(core == 0)
+    def _():
+        for j in range(2):
+            line_second(j).wait()
+            share_ring(1 + j).start()
+        stay().wait()
+        for j in range(3):
+            share_ring(j).wait_send()
+        for j in range(4):
+            share_line_in(j).wait_recv()
+
+    @pl.when(core == 1)
+    def _():
+        for j in range(3):
+            ring_second(j).wait()
+            share_line(1 + j).start()
+        stay_here().wait()
+        for j in range(4):
+            share_line(j).wait_send()
+        for j in range(3):
+            share_ring_in(j).wait_recv()
+
     for d in range(1, n_band):
         flag_copy(d).wait()
     total = flag[...]
     for d in range(1, n_band):
         total = total + flag_got[lax.rem(b + d, n_band)]
-    flag_ref[...] = total
-
-    @pl.when(core == 0)
-    def _():
-        for j in range(3):
-            ring_first(j).wait()
-        for j in range(2):
-
-            def fill(p, carry):
-                cell = at_index(1, p, FINAL_RING)
-                for m in range(PACK // 8):
-                    send2[p, 8 * m : 8 * m + 8, :] = ring_got[cell, 8 * m : 8 * m + 8, :]
-                return carry
-
-            lax.fori_loop(j * half, (j + 1) * half, fill, 0)
-            line_second(j).start()
-        share_ring(0).start()
-        stay = pltpu.make_async_copy(ring_got, final.at[pl.ds(0, FINAL_RING)], local_sem.at[1])
-        stay.start()
-        for j in range(2):
-            line_second(j).wait()
-            share_ring(1 + j).start()
-        stay.wait()
-        for j in range(3):
-            share_ring(j).wait_send()
-        for j in range(4):
-            share_line_in(j).wait_recv()
-
-    @pl.when(core == 1)
-    def _():
-        line_first().wait()
-        for j in range(4):
-            to = lax.rem(y + (STEPS[j] if j < 3 else 0), RING)
-
-            def fill(p, carry, j=j, to=to):
-                index = at_index(1, to * RING_SECOND + p, 2 * CAP)
-                mine = index < CAP
-                here, there = jnp.minimum(index, CAP - 1), jnp.maximum(index - CAP, 0)
-                for m in range(PACK // 8):
-                    v = jnp.where(mine, own[here, 8 * m : 8 * m + 8, :], line_got[there, 8 * m : 8 * m + 8, :])
-                    if j < 3:
-                        send2[j * RING_SECOND + p, 8 * m : 8 * m + 8, :] = v
-                    else:
-                        final[FINAL_LINE + y * RING_SECOND + p, 8 * m : 8 * m + 8, :] = v
-                return carry
-
-            lax.fori_loop(0, RING_SECOND, fill, 0)
-            if j < 3:
-                ring_second(j).start()
-        share_line(0).start()
-        for j in range(3):
-            ring_second(j).wait()
-            share_line(1 + j).start()
-        for j in range(4):
-            share_line(j).wait_send()
-        for j in range(3):
-            share_ring_in(j).wait_recv()
+    flag_ref[0] = jnp.sum(total[0:1, :].astype(F32)).astype(jnp.int32)
+
+    keep.wait()
+    hand_on.wait()
+
+
+def place_kernel(table, final, result, got, made, in_sem, out_sem):
+    tiles, groups = VOX // 128, GROUP * MOST // 8
+
+    def load(p):
+        cell = jnp.clip(table[1, p] - 1, 0, FINAL - 1)
+        return pltpu.make_async_copy(final.at[cell], got.at[p], in_sem.at[p])
+
+    for p in range(GROUP * MOST):
+
+        @pl.when(table[1, p] > 0)
+        def _(p=p):
+            load(p).start()
+
+    def clear(i, carry):
+        made[pl.ds(pl.multiple_of(i * 216, 216), 216), :] = jnp.zeros((216, 128), F32)
+        return carry
+
+    lax.fori_loop(0, 3 * groups * tiles * 8 // 216, clear, 0)
+
+    def one(p, carry):
+        @pl.when(table[1, p] > 0)
+        def _():
+            load(p).wait()
+            for m in range(PACK // 8):
+                v = got[p, 8 * m : 8 * m + 8, :]
+                row = 8 * m
+                while row < min(8 * m + 8, ROWS):
+                    c, tile = row // tiles, row % tiles
+                    count = min(8 * m + 8, (c + 1) * tiles) - row
+                    start = ((c * groups + p // 8) * tiles + tile) * 8 + p % 8
+                    made[pl.ds(start, count, stride=8), :] = v[row - 8 * m : row - 8 * m + count]
+                    row = row + count
+
+        return carry
 
     stores = []
-    for t in range(GROUP * MOST // 8):
-
-        def choose(p, carry):
-            filled = table[2, p] > 0
-            cell = at_index(2, p, FINAL)
-            for m in range(PACK // 8):
-                chosen[p, 8 * m : 8 * m + 8, :] = jnp.where(filled, final[cell, 8 * m : 8 * m + 8, :], 0.0)
-            return carry
-
-        lax.fori_loop(8 * t, 8 * t + 8, choose, 0)
-        span = pl.ds(8 * t, 8)
-        stores.append(pltpu.make_async_copy(chosen.at[span], result_ref.at[span], out_sem.at[t]))
-        stores[-1].start()
-    keep.wait()
+    for t in range(groups):
+        lax.fori_loop(8 * t, 8 * t + 8, one, 0)
+        for c in range(3):
+            span = pl.ds((c * groups + t) * tiles * 8, tiles * 8)
+            stores.append(pltpu.make_async_copy(made.at[span], result.at[span], out_sem.at[3 * t + c]))
+            stores[-1].start()
     for copy in stores:
         copy.wait()
 
 
-def layout_kernel(slots, recv_ref, out_ref, got, made, in_sem, out_sem):
-    tiles = VOX // 128
-    spans = []
-    for c in range(3):
-        low = c * tiles // 8 * 8
-        high = min(-(-(c + 1) * tiles // 8) * 8, PACK)
-        spans.append((low, high))
-    loads = []
-    for c, (low, high) in enumerate(spans):
-        place = got.at[c, :, 0 : high - low, :]
-        loads.append(pltpu.make_async_copy(recv_ref.at[:, low:high, :], place, in_sem.at[c]))
-        loads[-1].start()
-    stores = []
-    for c, (low, _) in enumerate(spans):
-        loads[c].wait()
-        for t in range(slots // 8):
-
-            def column(j, carry):
-                v = got[c, 8 * t : 8 * t + 8, pl.ds(c * tiles - low + 4 * j, 4), :]
-                for s in range(4):
-                    made[c, 8 * t : 8 * t + 8, pl.ds(pl.multiple_of((4 * j + s) * 128, 128), 128)] = v[:, s, :]
-                return carry
-
-            lax.fori_loop(0, tiles // 4, column, 0)
-        stores.append(pltpu.make_async_copy(made.at[c], out_ref.at[c], out_sem.at[c]))
-        stores[-1].start()
-    for copy in stores:
-        copy.wait()
-
-
-def fast_layout(slots, result):
-    any_space = pl.BlockSpec(memory_space=pltpu.HBM)
-    return pl.pallas_call(
-        lambda *refs: layout_kernel(slots, *refs),
-        out_shape=jax.ShapeDtypeStruct((3, slots, VOX), F32),
-        in_specs=[any_space],
-        out_specs=any_space,
+def place(table, final):
+    hbm = pl.BlockSpec(memory_space=pltpu.HBM)
+    slots = GROUP * MOST
+    result = pl.pallas_call(
+        place_kernel,
+        out_shape=jax.ShapeDtypeStruct((3 * slots * VOX // 128, 128), F32),
+        in_specs=[pl.BlockSpec(memory_space=pltpu.SMEM), hbm],
+        out_specs=hbm,
         scratch_shapes=[
-            pltpu.VMEM((3, slots, 120, 128), F32),
-            pltpu.VMEM((3, slots, VOX), F32),
-            pltpu.SemaphoreType.DMA((3,)),
-            pltpu.SemaphoreType.DMA((3,)),
+            pltpu.VMEM((slots, PACK, 128), F32),
+            pltpu.VMEM((3 * slots * VOX // 128, 128), F32),
+            pltpu.SemaphoreType.DMA((slots,)),
+            pltpu.SemaphoreType.DMA((3 * slots // 8,)),
         ],
-        compiler_params=pltpu.CompilerParams(vmem_limit_bytes=32 * 2**20),
-        name="layout",
-    )(result)
+        compiler_params=pltpu.CompilerParams(vmem_limit_bytes=60 * 2**20),
+        name="place",
+    )(table, final)
+    return in_place(slots, result)
+
+
+def in_place(slots, result):
+    tiles = result.reshape(3, slots // 8, VOX // 128, 8, 128)
+    return tiles.transpose(0, 1, 3, 2, 4).reshape(3, slots, VOX)
 
 
 def send_all(workers, own, n_gore, slots):
@@ -666,16 +700,17 @@
     n = G * CAP
     vm, dma = pltpu.VMEM, pltpu.SemaphoreType.DMA
     workers = route.reshape(-1)
-    force, flag, result, own = pl.pallas_call(
+    force, flag, table, final, own = pl.pallas_call(
         lambda *refs: kernel(n_gore, n_band, *refs),
         out_shape=(
             jax.ShapeDtypeStruct((3, nodes_g, nodes_b), F32),
+            jax.ShapeDtypeStruct((1,), jnp.int32),
             jax.ShapeDtypeStruct((8, 128), jnp.int32),
-            jax.ShapeDtypeStruct((slots, PACK, 128), F32),
+            jax.ShapeDtypeStruct((FINAL, PACK, 128), F32),
             jax.ShapeDtypeStruct((CAP, PACK, 128), F32),
         ),
         in_specs=[hbm] * 11,
-        out_specs=(vmem, vmem, hbm, hbm),
+        out_specs=(vmem, pl.BlockSpec(memory_space=pltpu.SMEM), hbm, hbm, hbm),
         scratch_shapes=[
             pltpu.SMEM((CAP,), jnp.int32),
             pltpu.SMEM((CAP,), jnp.int32),
@@ -707,13 +742,14 @@
             vm((n_band, 8, 128), jnp.int32),
             vm((8, 128), jnp.int32),
             pltpu.SMEM((8, 128), jnp.int32),
+            vm((8, 128), jnp.int32),
+            pltpu.SMEM((8, 128), jnp.int32),
             vm((CAP, PACK, 128), F32),
             vm((3 * RING_FIRST, PACK, 128), F32),
             vm((3 * RING_SECOND, PACK, 128), F32),
             vm((FINAL_RING, PACK, 128), F32),
             vm((LINE_FIRST, PACK, 128), F32),
-            vm((FINAL, PACK, 128), F32),
-            vm((slots, PACK, 128), F32),
+            vm((RING_SECOND, PACK, 128), F32),
             dma((11,)),
             dma((8,)),
             dma((8,)),
@@ -721,7 +757,7 @@
             dma((n_gore,)),
             dma((n_band,)),
             dma((n_band,)),
-            dma,
+            dma((3,)),
             dma((3,)),
             dma((3,)),
             dma((3,)),
@@ -729,10 +765,9 @@
             dma((4,)),
             dma((4,)),
             dma((2,)),
-            dma((slots // 8,)),
         ],
         compiler_params=pltpu.CompilerParams(
-            collective_id=0, has_side_effects=True, vmem_limit_bytes=56 * 2**20
+            collective_id=0, has_side_effects=True, vmem_limit_bytes=60 * 2**20
         ),
         name="cells",
     )(
@@ -749,10 +784,10 @@
         jnp.asarray(weight),
     )
     cell_strain = lax.cond(
-        flag[0, 0] == 0,
-        lambda result, own, workers: fast_layout(slots, result),
-        lambda result, own, workers: send_all(workers, own, n_gore, slots),
-        result, own, workers,
+        flag[0] == 0,
+        lambda table, final, own, workers: place(table, final),
+        lambda table, final, own, workers: send_all(workers, own, n_gore, slots),
+        table, final, own, workers,
     )
     return force, cell_strain.transpose(1, 0, 2)
 

time: 175 us -> 169 us (0.966)
  Pallas kernels: 79 us -> 74 us
    pallas_call x1, Pallas kernels: 79 us -> 74 us  [local(): pl.pallas_call(lambda *refs: kernel(n_gore, n_band, *refs), out_shape=(ja...]
where the time goes in v3:
time: 169 us
  Pallas kernels  74 us (44%)
  blocking collectives  65.4 us (39%)
  local copies, waits for them, and re-layouts  25.8 us (15%)
  other arithmetic  2.25 us (1%)
    pallas_call x1, Pallas kernels, local(): pl.pallas_call(lambda *refs: kernel(n_gore, n_band, *refs), out_shape=(ja...  74 us
    all_to_all x1, blocking collectives, send_all(): lax.all_to_all(outgoing.reshape(n_gore, MOST, 3, VOX), 'gore', split_axis...  65.4 us
    reshape x1, local copies, waits for them, and re-layouts, send_all(): return arrived.reshape(slots, 3, VOX).transpose(1, 0, 2)  7.04 us
    reshape x1, local copies, waits for them, and re-layouts, send_all(): outgoing.reshape(n_gore, MOST, 3, VOX)  5.74 us
    scatter x1, local copies, waits for them, and re-layouts, send_all(): outgoing = jnp.zeros((slots, 3, VOX), F32).at[slot_index].set(states)  5.07 us
    another operation x1, local copies, waits for them, and re-layouts  3.8 us

profile of v3, /device:TPU:1, one launch (start us, length us, event | category | flops | bytes accessed | tf_op | source)
XLA Modules:
  0.0 168.8 jit_solution(7423753317181642818)
XLA Ops:
  0.6 74.0 %cells.1 = (f32[3,128,256]{2,1,0:T(8,128)}, s32[1]{0:T(128)}, s32[8,128]{1,0:T(8,128)S(1)}, f32[54,328,128]{2,1,0:T(8,128)}, f32[8,328,128]{2,1,0:T(8,128)S(1)}) custom-call(s32[8]{0:T(128)} %refs_0_.1, s32[8]{0:T(128)} %bitcast.24, f32[3,128,256]{2,1,0:T(8,128)} %refs_2_.1, f32[128,256]{1,0:T(8,128)} %refs_3_.1, f32[128,256]{1,0:T(8,128)} %refs_4_.1, ...), custom_call_target="tpu_custom_call" | custom-call | tf_op jit(solution)/shard_map/cells/pallas_call | solution.py:703
  75.1 0.0 copy-start
  75.2 92.9 %conditional.1 = (f32[3,32,13824]{2,1,0:T(8,128)}) conditional(s32[]{:T(128)} %bitcast.11, (s32[8]{0:T(128)}, s32[8,1]{0,1:T(1,128)}, f32[8,328,128]{2,1,0:T(8,128)S(1)}) %tuple.21, (s32[8,128]{1,0:T(8,128)S(1)}, f32[54,328,128]{2,1,0:T(8,128)}) %tuple.15), branch_computations={%region_0.4_spmd, %region_4.5_spmd} | conditional | flops 1824 | bytes 54413552 | solution.py:786
  75.3 0.7 fusion
  76.1 0.8 select_reduce_fusion
  76.9 0.7 reshape.36
  77.6 0.7 compare_select_fusion
  78.3 3.8 %broadcast.10 = f32[32,3,13824]{2,1,0:T(4,128)} broadcast(f32[]{:T(128)} %constant.9.clone), dimensions={} | broadcast | bytes 5308420 | tf_op jit(solution)/shard_map/broadcast.4
  82.1 5.1 %scatter_fusion = f32[32,3,13824]{2,1,0:T(4,128)} fusion(f32[32,3,13824]{2,1,0:T(4,128)} %broadcast.10, s32[8]{0:T(128)S(1)} %compare_select_fusion, f32[8,3,13824]{2,1,0:T(4,128)S(1)} %reshape.36), kind=kCustom, calls=%fused_computation | custom fusion | bytes 3981344 | tf_op jit(solution)/shard_map/cond/branch_0_fun/scatter | solution.py:687
  87.1 5.7 %copy.25 = f32[16,2,3,13824]{3,1,2,0:T(2,128)S(1)} copy(f32[16,2,3,13824]{3,2,1,0:T(4,128)} %bitcast.17) | data formatting | bytes 10616832 | tf_op jit(solution)/shard_map/cond/branch_0_fun/reshape | solution.py:689
  92.9 65.4 %all_to_all.4 = f32[16,2,3,13824]{3,1,2,0:T(2,128)S(1)} all-to-all(f32[16,2,3,13824]{3,1,2,0:T(2,128)S(1)} %copy.25), channel_id=1, replica_groups=mesh['gore'=16,'band'=8] {'gore'}, dimensions={0} | all-to-all | bytes 10616832 | tf_op jit(solution)/shard_map/cond/branch_0_fun/all_to_all | solution.py:688
  158.2 2.8 %copy.26 = f32[16,2,3,13824]{3,1,0,2:T(2,128)} copy(f32[16,2,3,13824]{3,1,2,0:T(2,128)S(1)} %all_to_all.4) | data formatting | bytes 10616832 | tf_op jit(solution)/shard_map/cond/branch_0_fun/all_to_all | solution.py:688
  161.0 7.0 %reshape.24 = f32[32,3,13824]{2,0,1:T(8,128)} reshape(f32[16,2,3,13824]{3,1,0,2:T(2,128)} %copy.26) | data formatting | bytes 10616832 | tf_op jit(solution)/shard_map/cond/branch_0_fun/reshape | solution.py:691
  168.0 0.0 copy-done
  168.0 0.7 copy.33
  (1 shorter events, 0.0 us)
Async XLA Ops:
  75.1 92.9 %copy-start = (f32[3,128,256]{2,1,0:T(8,128)S(1)}, f32[3,128,256]{2,1,0:T(8,128)}, u32[]{:S(2)}) copy-start(f32[3,128,256]{2,1,0:T(8,128)} %get-tuple-element.32) | copy-start | bytes 1179652

commit v4 on v3

--- a/solution.py
+++ b/solution.py
@@ -19,10 +19,11 @@
 PACK = 328
 RING, LINE, CORE = 4, 2, 2
 GROUP = RING * LINE * CORE
-RING_FIRST, LINE_SECOND, LINE_FIRST, RING_SECOND = 5, 10, 8, 6
+RING_FIRST, LINE_NEAR, LINE_FAR, LINE_FIRST, RING_SECOND = 5, 9, 3, 8, 6
 STEPS = (1, 3, 2)
 FINAL_RING = RING * RING_FIRST
-FINAL_LINE = FINAL_RING + LINE_SECOND
+FINAL_LINE = FINAL_RING + LINE_NEAR + LINE_FAR
+NEAR = (RING - 1) * RING_FIRST
 FINAL = FINAL_LINE + RING * RING_SECOND
 MESH = pl.DeviceIdType.MESH
 F32 = jnp.float32
@@ -124,21 +125,26 @@
         place, index = to_column(place.astype(F32)), to_column(index.astype(F32) + 1.0)
         return jnp.sum(jnp.where(place == column, index, 0.0), axis=0, keepdims=True).astype(jnp.int32)
 
+    ahead = (from_y + RING - to_y) & (RING - 1)
+    block = jnp.where(ahead == 3, 1, jnp.where(ahead == 1, 2, jnp.where(ahead == 2, 3, 0)))
+    far = jnp.where(ahead == 2, 1, 0)
     ring_first = rank(source * RING + to_y)
     line_first = rank(jnp.where(crossing, source, alone))
     place1_ring = jnp.where(own, to_y * RING_FIRST + ring_first, -1)
     place1 = jnp.where(at_ring, place1_ring, jnp.where(own & crossing, line_first, -1))
 
     def later():
-        line_second = rank(jnp.where(first & crossing, from_z * RING + to_y, alone))
+        line_second = rank(jnp.where(first & crossing, (from_z * RING + to_y) * 2 + far, alone))
+        line_over = line_second >= LINE_NEAR + far * (LINE_FAR - LINE_NEAR)
+        line_second = line_second + far * LINE_NEAR
         ring_second = rank(jnp.where(first, alone, (from_y * RING + to_y) * LINE + to_z))
         slot = rank(source * GROUP + to)
-        over = first & ((ring_first >= RING_FIRST) | (crossing & (line_second >= LINE_SECOND)))
+        over = first & ((ring_first >= RING_FIRST) | (crossing & line_over))
         over = over | (jnp.logical_not(first) & (ring_second >= RING_SECOND))
         place2_ring = jnp.where(mine & crossing & (from_z == z) & (to_y == y), line_second, -1)
         place2_line = jnp.where(mine & (from_y == y) & (to_z == z), to_y * RING_SECOND + ring_second, -1)
         place2 = jnp.where(at_ring, place2_ring, place2_line)
-        from_ring = from_y * RING_FIRST + ring_first
+        from_ring = block * RING_FIRST + ring_first
         from_line = jnp.where(from_z == z, cell, CAP + line_first)
         index2 = jnp.where(at_ring, from_ring, from_line)
         place3 = jnp.where(to == g, source * MOST + slot, -1)
@@ -160,7 +166,7 @@
     halo_g, halo_b, got_g, got_b, slopes, strain_s,
     e_s, w_s, s_pad, d_s, x_s, f_s, cells,
     names, names_got, flag, flag_got, hop1_v, hop1_table, table_v, table,
-    own, send1, send2, ring_got, line_got, here_got,
+    own, send1, send2, ring_got, ring_far, line_got, here_got,
     in_sem, halo_send, halo_recv, name_send, name_recv, flag_send, flag_recv, table_sem,
     hop1_send, hop1_recv, hop2_send, hop2_recv, share_send, share_recv, local_sem,
 ):
@@ -393,27 +399,29 @@
     def ring_first(j):
         to = lax.rem(y + STEPS[j], RING)
         n = RING_FIRST
-        return hop(one, j, send1.at[pl.ds(j * n, n)], ring_got.at[pl.ds(y * n, n)], to, z, 0)
+        place = ring_got.at[pl.ds((j + 1) * n, n)] if j < 2 else ring_far
+        return hop(one, j, send1.at[pl.ds(j * n, n)], place, to, z, 0)
 
     def line_first():
         return hop(one, 0, send1.at[pl.ds(0, LINE_FIRST)], line_got, y, 1 - z, 1)
 
-    half = LINE_SECOND // 2
+    line_spans = ((0, LINE_NEAR), (LINE_NEAR, LINE_FAR))
 
     def line_second(j):
-        span = pl.ds(j * half, half)
-        return hop(two, j, send2.at[span], final.at[pl.ds(FINAL_RING + j * half, half)], y, 1 - z, 0)
+        low, n = line_spans[j]
+        return hop(two, j, send2.at[pl.ds(low, n)], final.at[pl.ds(FINAL_RING + low, n)], y, 1 - z, 0)
 
     def ring_second(j):
         to = lax.rem(y + STEPS[j], RING)
         n = RING_SECOND
         return hop(two, j, send2.at[pl.ds(j * n, n)], final.at[pl.ds(FINAL_LINE + y * n, n)], to, z, 1)
 
-    def share_ring(j):
-        if j == 0:
-            return hop(three, 0, ring_got, final.at[pl.ds(0, FINAL_RING)], y, z, 1)
-        span = final.at[pl.ds(FINAL_RING + (j - 1) * half, half)]
-        return hop(three, j, span, span, y, z, 1)
+    ring_spans = ((0, NEAR), (NEAR, RING_FIRST)) + tuple((FINAL_RING + low, n) for low, n in line_spans)
+
+    def share_ring(j, to=1):
+        low, n = ring_spans[j]
+        span = final.at[pl.ds(low, n)]
+        return hop(three, j, (ring_got, ring_far, span, span)[j], span, y, z, to)
 
     def share_line(j):
         from_y = y if j == 0 else lax.rem(y + RING - STEPS[j - 1], RING)
@@ -426,9 +434,7 @@
         return hop(three, j, span, span, y, z, 1)
 
     def share_ring_in(j):
-        low, n = (0, FINAL_RING) if j == 0 else (FINAL_RING + (j - 1) * half, half)
-        span = final.at[pl.ds(low, n)]
-        return hop(three, j, span, span, y, z, 0)
+        return share_ring(j, 0)
 
     @pl.when(core == 0)
     def _():
@@ -442,7 +448,7 @@
                     if j < 3:
                         send1[j * RING_FIRST + p, 8 * m : 8 * m + 8, :] = v
                     else:
-                        ring_got[y * RING_FIRST + p, 8 * m : 8 * m + 8, :] = v
+                        ring_got[p, 8 * m : 8 * m + 8, :] = v
                 return carry
 
             lax.fori_loop(0, RING_FIRST, fill, 0)
@@ -517,25 +523,29 @@
         span = pl.ds(FINAL_LINE + y * RING_SECOND, RING_SECOND)
         return pltpu.make_async_copy(here_got, final.at[span], local_sem.at[1])
 
-    def stay():
-        return pltpu.make_async_copy(ring_got, final.at[pl.ds(0, FINAL_RING)], local_sem.at[1])
+    def stay(j):
+        low, n = ring_spans[j]
+        return pltpu.make_async_copy((ring_got, ring_far)[j], final.at[pl.ds(low, n)], local_sem.at[1 + j])
 
     @pl.when(core == 0)
     def _():
-        for j in range(3):
-            ring_first(j).wait()
         for j in range(2):
-
-            def fill(p, carry):
+            for i in ((0, 1), (2,))[j]:
+                ring_first(i).wait()
+
+            def fill(p, carry, j=j):
                 cell = at_index(table, 0, p, FINAL_RING)
+                held = ring_got if j == 0 else ring_far
+                cell = jnp.clip(cell - j * NEAR, 0, held.shape[0] - 1)
                 for m in range(PACK // 8):
-                    send2[p, 8 * m : 8 * m + 8, :] = ring_got[cell, 8 * m : 8 * m + 8, :]
+                    send2[p, 8 * m : 8 * m + 8, :] = held[cell, 8 * m : 8 * m + 8, :]
                 return carry
 
-            lax.fori_loop(j * half, (j + 1) * half, fill, 0)
+            low, n = line_spans[j]
+            lax.fori_loop(low, low + n, fill, 0)
             line_second(j).start()
-        share_ring(0).start()
-        stay().start()
+            share_ring(j).start()
+            stay(j).start()
 
     @pl.when(core == 1)
     def _():
@@ -579,9 +589,10 @@
     def _():
         for j in range(2):
             line_second(j).wait()
-            share_ring(1 + j).start()
-        stay().wait()
-        for j in range(3):
+            share_ring(2 + j).start()
+        for j in range(2):
+            stay(j).wait()
+        for j in range(4):
             share_ring(j).wait_send()
         for j in range(4):
             share_line_in(j).wait_recv()
@@ -594,7 +605,7 @@
         stay_here().wait()
         for j in range(4):
             share_line(j).wait_send()
-        for j in range(3):
+        for j in range(4):
             share_ring_in(j).wait_recv()
 
     for d in range(1, n_band):
@@ -747,7 +758,8 @@
             vm((CAP, PACK, 128), F32),
             vm((3 * RING_FIRST, PACK, 128), F32),
             vm((3 * RING_SECOND, PACK, 128), F32),
-            vm((FINAL_RING, PACK, 128), F32),
+            vm((NEAR, PACK, 128), F32),
+            vm((RING_FIRST, PACK, 128), F32),
             vm((LINE_FIRST, PACK, 128), F32),
             vm((RING_SECOND, PACK, 128), F32),
             dma((11,)),
@@ -764,7 +776,7 @@
             dma((3,)),
             dma((4,)),
             dma((4,)),
-            dma((2,)),
+            dma((3,)),
         ],
         compiler_params=pltpu.CompilerParams(
             collective_id=0, has_side_effects=True, vmem_limit_bytes=60 * 2**20

time: 169 us -> 81.5 us (0.48)
  blocking collectives: 65.4 us -> 0 us
  local copies, waits for them, and re-layouts: 25.8 us -> 0.75 us
  Pallas kernels: 74 us -> 79 us
  other arithmetic: 2.25 us -> 0 us
    all_to_all x1 -> x0, blocking collectives: 65.4 us -> none  [send_all(): lax.all_to_all(outgoing.reshape(n_gore, MOST, 3, VOX), 'gore', split_axis...]
    reshape x3 -> x0, local copies, waits for them, and re-layouts: 13.4 us -> none  [the longest x1 7.04 us: send_all(): return arrived.reshape(slots, 3, VOX).transpose(1, 0, 2)]
    scatter x1 -> x0, local copies, waits for them, and re-layouts: 5.07 us -> none  [send_all(): outgoing = jnp.zeros((slots, 3, VOX), F32).at[slot_index].set(states)]
    pallas_call x0 -> x1, Pallas kernels: none -> 4.48 us  [place(): pl.pallas_call(place_kernel, out_shape=jax.ShapeDtypeStruct((3 * slots *...]
    another operation x1 -> x0, local copies, waits for them, and re-layouts: 3.8 us -> none
    all_to_all x1 -> x0, local copies, waits for them, and re-layouts: 2.75 us -> none  [send_all(): lax.all_to_all(outgoing.reshape(n_gore, MOST, 3, VOX), 'gore', split_axis...]
where the time goes in v4:
time: 81.5 us; the launch traced here: 81.4 us
  Pallas kernels  79 us (97%)
  between operations  1.34 us (2%)
    pallas_call x1, Pallas kernels, local(): pl.pallas_call(lambda *refs: kernel(n_gore, n_band, *refs), out_shape=(ja...  74.6 us
    pallas_call x1, Pallas kernels, place(): pl.pallas_call(place_kernel, out_shape=jax.ShapeDtypeStruct((3 * slots *...  4.48 us

profile of v4, /device:TPU:1, one launch (start us, length us, event | category | flops | bytes accessed | tf_op | source)
XLA Modules:
  0.0 81.4 jit_solution(2855386763131185212)
XLA Ops:
  0.6 74.6 %cells.1 = (f32[3,128,256]{2,1,0:T(8,128)}, s32[1]{0:T(128)}, s32[8,128]{1,0:T(8,128)S(1)}, f32[56,328,128]{2,1,0:T(8,128)}, f32[8,328,128]{2,1,0:T(8,128)S(1)}) custom-call(s32[8]{0:T(128)} %refs_0_.1, s32[8]{0:T(128)} %bitcast.24, f32[3,128,256]{2,1,0:T(8,128)} %refs_2_.1, f32[128,256]{1,0:T(8,128)} %refs_3_.1, f32[128,256]{1,0:T(8,128)} %refs_4_.1, ...), custom_call_target="tpu_custom_call" | custom-call | tf_op jit(solution)/shard_map/cells/pallas_call | solution.py:714
  75.9 0.0 copy-start
  75.9 4.7 %conditional.1 = (f32[3,32,13824]{2,1,0:T(8,128)}) conditional(s32[]{:T(128)} %bitcast.11, (s32[8]{0:T(128)}, s32[8,1]{0,1:T(1,128)}, f32[8,328,128]{2,1,0:T(8,128)S(1)}) %tuple.21, (s32[8,128]{1,0:T(8,128)S(1)}, f32[56,328,128]{2,1,0:T(8,128)}) %tuple.15), branch_computations={%region_0.4_spmd, %region_4.5_spmd} | conditional | flops 1824 | bytes 54413552 | solution.py:798
  76.1 4.5 %place.1 = f32[10368,128]{1,0:T(8,128)} custom-call(s32[8,128]{1,0:T(8,128)S(1)} %get-tuple-element.16.table, f32[56,328,128]{2,1,0:T(8,128)} %get-tuple-element.17.final), custom_call_target="tpu_custom_call" | custom-call | tf_op jit(solution)/shard_map/cond/branch_1_fun/place/pallas_call | solution.py:671
  80.6 0.0 copy-done
  80.6 0.7 copy.33
Async XLA Ops:
  75.9 4.7 %copy-start = (f32[3,128,256]{2,1,0:T(8,128)S(1)}, f32[3,128,256]{2,1,0:T(8,128)}, u32[]{:S(2)}) copy-start(f32[3,128,256]{2,1,0:T(8,128)} %get-tuple-element.32) | copy-start | bytes 1179652

commit v5 on v4

--- a/solution.py
+++ b/solution.py
@@ -256,7 +256,7 @@
         return tuple(out)
 
     zero = jnp.zeros((CAP, PLANE), F32)
-    sums = lax.fori_loop(0, G // 2, load_states, (zero, zero, zero), unroll=2)
+    sums = lax.fori_loop(0, G // 2, load_states, (zero, zero, zero), unroll=True)
     means = [jnp.sum(s, axis=1, keepdims=True) * (1.0 / VOX) for s in sums]
 
     for d in range(1, n_gore):
@@ -341,7 +341,7 @@
             d_s[pl.ds(at, 16), :] = diff_upper(s[1]) + diff_lower(s[2], low)
             return carry
 
-        lax.fori_loop(0, G // 2, law, 0, unroll=6)
+        lax.fori_loop(0, G // 2, law, 0, unroll=True)
         s_pad[0:8, :] = s_pad[G * 8 : G * 8 + 8, :]
         s_pad[G * 8 + 8 :, :] = s_pad[8:16, :]
 
@@ -353,7 +353,7 @@
             x_s[pl.ds(G * CAP + at, 16), :] = rest
             return carry
 
-        lax.fori_loop(0, G // 2, source, 0, unroll=6)
+        lax.fori_loop(0, G // 2, source, 0, unroll=True)
         spectrum = lines(planes(x_s[...]))
         weight = jnp.broadcast_to(weight_ref[...], (G, CAP, PLANE)).reshape(G * CAP, PLANE)
         back = lines(spectrum * weight)
@@ -375,7 +375,7 @@
             out.append(sums[c] + s[c][0:8] + s[c][8:16])
         return tuple(out)
 
-    sums = lax.fori_loop(0, G // 2, finish, (zero, zero, zero), unroll=2)
+    sums = lax.fori_loop(0, G // 2, finish, (zero, zero, zero), unroll=True)
     point_stress = [jnp.sum(s, axis=1, keepdims=True) * (1.0 / VOX) for s in sums]
 
     cells[ROWS * CAP :, :] = jnp.zeros((PACK * CAP - ROWS * CAP, 128), F32)
@@ -405,33 +405,40 @@
     def line_first():
         return hop(one, 0, send1.at[pl.ds(0, LINE_FIRST)], line_got, y, 1 - z, 1)
 
-    line_spans = ((0, LINE_NEAR), (LINE_NEAR, LINE_FAR))
+    line_spans = ((0, 5), (5, LINE_NEAR - 5), (LINE_NEAR, LINE_FAR))
 
     def line_second(j):
         low, n = line_spans[j]
         return hop(two, j, send2.at[pl.ds(low, n)], final.at[pl.ds(FINAL_RING + low, n)], y, 1 - z, 0)
 
-    def ring_second(j):
+    half = RING_SECOND // 3
+    pieces = tuple((j, h) for h in range(3) for j in range(3))
+
+    def ring_second(i):
+        j, h = pieces[i]
         to = lax.rem(y + STEPS[j], RING)
-        n = RING_SECOND
-        return hop(two, j, send2.at[pl.ds(j * n, n)], final.at[pl.ds(FINAL_LINE + y * n, n)], to, z, 1)
+        source = send2.at[pl.ds(j * RING_SECOND + h * half, half)]
+        return hop(two, i, source, final.at[pl.ds(FINAL_LINE + y * RING_SECOND + h * half, half)], to, z, 1)
 
     ring_spans = ((0, NEAR), (NEAR, RING_FIRST)) + tuple((FINAL_RING + low, n) for low, n in line_spans)
 
     def share_ring(j, to=1):
         low, n = ring_spans[j]
         span = final.at[pl.ds(low, n)]
-        return hop(three, j, (ring_got, ring_far, span, span)[j], span, y, z, to)
-
-    def share_line(j):
-        from_y = y if j == 0 else lax.rem(y + RING - STEPS[j - 1], RING)
-        span = final.at[pl.ds(FINAL_LINE + from_y * RING_SECOND, RING_SECOND)]
-        return hop(three, j, here_got if j == 0 else span, span, y, z, 0)
-
-    def share_line_in(j):
-        from_y = y if j == 0 else lax.rem(y + RING - STEPS[j - 1], RING)
-        span = final.at[pl.ds(FINAL_LINE + from_y * RING_SECOND, RING_SECOND)]
-        return hop(three, j, span, span, y, z, 1)
+        return hop(three, j, (ring_got, ring_far, span, span, span)[j], span, y, z, to)
+
+    def share_line(i, to=0):
+        if i == 0:
+            span, source = pl.ds(FINAL_LINE + y * RING_SECOND, RING_SECOND), here_got
+        else:
+            j, h = pieces[i - 1]
+            from_y = lax.rem(y + RING - STEPS[j], RING)
+            span = pl.ds(FINAL_LINE + from_y * RING_SECOND + h * half, half)
+            source = final.at[span]
+        return hop(three, i, source, final.at[span], y, z, to)
+
+    def share_line_in(i):
+        return share_line(i, 1)
 
     def share_ring_in(j):
         return share_ring(j, 0)
@@ -541,16 +548,18 @@
                     send2[p, 8 * m : 8 * m + 8, :] = held[cell, 8 * m : 8 * m + 8, :]
                 return carry
 
-            low, n = line_spans[j]
-            lax.fori_loop(low, low + n, fill, 0)
-            line_second(j).start()
+            for k in ((0, 1), (2,))[j]:
+                low, n = line_spans[k]
+                lax.fori_loop(low, low + n, fill, 0)
+                line_second(k).start()
             share_ring(j).start()
             stay(j).start()
 
     @pl.when(core == 1)
     def _():
         line_first().wait()
-        for j in range(4):
+        for i in range(12):
+            j, h = pieces[i] if i < 9 else (3, i - 9)
             to = lax.rem(y + (STEPS[j] if j < 3 else 0), RING)
 
             def fill(p, carry, j=j, to=to):
@@ -565,9 +574,9 @@
                         here_got[p, 8 * m : 8 * m + 8, :] = v
                 return carry
 
-            lax.fori_loop(0, RING_SECOND, fill, 0)
+            lax.fori_loop(h * half, (h + 1) * half, fill, 0)
             if j < 3:
-                ring_second(j).start()
+                ring_second(i).start()
         share_line(0).start()
         stay_here().start()
 
@@ -587,25 +596,25 @@
         force_ref[c] = value
     @pl.when(core == 0)
     def _():
-        for j in range(2):
+        for j in range(3):
             line_second(j).wait()
             share_ring(2 + j).start()
         for j in range(2):
             stay(j).wait()
-        for j in range(4):
+        for j in range(5):
             share_ring(j).wait_send()
-        for j in range(4):
-            share_line_in(j).wait_recv()
+        for i in range(10):
+            share_line_in(i).wait_recv()
 
     @pl.when(core == 1)
     def _():
-        for j in range(3):
-            ring_second(j).wait()
-            share_line(1 + j).start()
+        for i in range(9):
+            ring_second(i).wait()
+            share_line(1 + i).start()
         stay_here().wait()
-        for j in range(4):
-            share_line(j).wait_send()
-        for j in range(4):
+        for i in range(10):
+            share_line(i).wait_send()
+        for j in range(5):
             share_ring_in(j).wait_recv()
 
     for d in range(1, n_band):
@@ -772,10 +781,10 @@
             dma((3,)),
             dma((3,)),
             dma((3,)),
-            dma((3,)),
-            dma((3,)),
-            dma((4,)),
-            dma((4,)),
+            dma((9,)),
+            dma((9,)),
+            dma((10,)),
+            dma((10,)),
             dma((3,)),
         ],
         compiler_params=pltpu.CompilerParams(

time: 81.5 us -> 76.2 us (0.935)
  Pallas kernels: 79 us -> 73.7 us
    pallas_call x1, Pallas kernels: 74.6 us -> 69.6 us  [local(): pl.pallas_call(lambda *refs: kernel(n_gore, n_band, *refs), out_shape=(ja...]
where the time goes in v5:
time: 76.2 us; the launch traced here: 76 us
  Pallas kernels  73.7 us (97%)
  between operations  1.34 us (2%)
    pallas_call x1, Pallas kernels, local(): pl.pallas_call(lambda *refs: kernel(n_gore, n_band, *refs), out_shape=(ja...  69.6 us
    pallas_call x1, Pallas kernels, place(): pl.pallas_call(place_kernel, out_shape=jax.ShapeDtypeStruct((3 * slots *...  4.08 us

profile of v5, /device:TPU:1, one launch (start us, length us, event | category | flops | bytes accessed | tf_op | source)
XLA Modules:
  0.0 76.0 jit_solution(1717302552772449343)
XLA Ops:
  0.6 69.6 %cells.1 = (f32[3,128,256]{2,1,0:T(8,128)}, s32[1]{0:T(128)}, s32[8,128]{1,0:T(8,128)S(1)}, f32[56,328,128]{2,1,0:T(8,128)}, f32[8,328,128]{2,1,0:T(8,128)S(1)}) custom-call(s32[8]{0:T(128)} %refs_0_.1, s32[8]{0:T(128)} %bitcast.24, f32[3,128,256]{2,1,0:T(8,128)} %refs_2_.1, f32[128,256]{1,0:T(8,128)} %refs_3_.1, f32[128,256]{1,0:T(8,128)} %refs_4_.1, ...), custom_call_target="tpu_custom_call" | custom-call | tf_op jit(solution)/shard_map/cells/pallas_call | solution.py:723
  70.9 0.0 copy-start
  70.9 4.3 %conditional.1 = (f32[3,32,13824]{2,1,0:T(8,128)}) conditional(s32[]{:T(128)} %bitcast.11, (s32[8]{0:T(128)}, s32[8,1]{0,1:T(1,128)}, f32[8,328,128]{2,1,0:T(8,128)S(1)}) %tuple.21, (s32[8,128]{1,0:T(8,128)S(1)}, f32[56,328,128]{2,1,0:T(8,128)}) %tuple.15), branch_computations={%region_0.4_spmd, %region_4.5_spmd} | conditional | flops 1824 | bytes 54413552 | solution.py:807
  71.2 4.1 %place.1 = f32[10368,128]{1,0:T(8,128)} custom-call(s32[8,128]{1,0:T(8,128)S(1)} %get-tuple-element.16.table, f32[56,328,128]{2,1,0:T(8,128)} %get-tuple-element.17.final), custom_call_target="tpu_custom_call" | custom-call | tf_op jit(solution)/shard_map/cond/branch_1_fun/place/pallas_call | solution.py:680
  75.3 0.0 copy-done
  75.3 0.7 copy.33
Async XLA Ops:
  70.9 4.3 %copy-start = (f32[3,128,256]{2,1,0:T(8,128)S(1)}, f32[3,128,256]{2,1,0:T(8,128)}, u32[]{:S(2)}) copy-start(f32[3,128,256]{2,1,0:T(8,128)} %get-tuple-element.32) | copy-start | bytes 1179652

commit v6 on v5

--- a/solution.py
+++ b/solution.py
@@ -308,8 +308,11 @@
         else:
             middle = f_s[pl.ds(at + 8, 16), :]
             e[0] = e[0] + 0.5 * (f_s[pl.ds(at + 16, 16), :] - f_s[pl.ds(at, 16), :])
-            e[1] = e[1] + 0.5 * diff_upper(middle)
-            e[2] = e[2] + 0.5 * diff_lower(middle, low)
+            after, before = shifted(middle, G), shifted(middle, -G)
+            e[1] = e[1] + 0.5 * (after - before)
+            forward = shifted(jnp.where(low == 0, before, middle), 1)
+            backward = shifted(jnp.where(low == G - 1, after, middle), -1)
+            e[2] = e[2] + 0.5 * (forward - backward)
         size = e[0] * e[0] + e[1] * e[1] + e[2] * e[2]
         factor = w_s[pl.ds(at, 16), :] * (1.5 - 0.5 / (1.0 + size))
         return at, e, [factor * v for v in e]

time: 76.2 us -> 75.8 us (level)
  no operation moved by 1% of the time
where the time goes in v6:
time: 75.8 us; the launch traced here: 75.5 us
  Pallas kernels  73.1 us (96%)
  between operations  1.34 us (2%)
    pallas_call x1, Pallas kernels, local(): pl.pallas_call(lambda *refs: kernel(n_gore, n_band, *refs), out_shape=(ja...  69.1 us
    pallas_call x1, Pallas kernels, place(): pl.pallas_call(place_kernel, out_shape=jax.ShapeDtypeStruct((3 * slots *...  4.03 us

profile of v6, /device:TPU:1, one launch (start us, length us, event | category | flops | bytes accessed | tf_op | source)
XLA Modules:
  0.0 75.5 jit_solution(4123651694958280575)
XLA Ops:
  0.6 69.1 %cells.1 = (f32[3,128,256]{2,1,0:T(8,128)}, s32[1]{0:T(128)}, s32[8,128]{1,0:T(8,128)S(1)}, f32[56,328,128]{2,1,0:T(8,128)}, f32[8,328,128]{2,1,0:T(8,128)S(1)}) custom-call(s32[8]{0:T(128)} %refs_0_.1, s32[8]{0:T(128)} %bitcast.24, f32[3,128,256]{2,1,0:T(8,128)} %refs_2_.1, f32[128,256]{1,0:T(8,128)} %refs_3_.1, f32[128,256]{1,0:T(8,128)} %refs_4_.1, ...), custom_call_target="tpu_custom_call" | custom-call | tf_op jit(solution)/shard_map/cells/pallas_call | solution.py:726
  70.4 0.0 copy-start
  70.4 4.3 %conditional.1 = (f32[3,32,13824]{2,1,0:T(8,128)}) conditional(s32[]{:T(128)} %bitcast.11, (s32[8]{0:T(128)}, s32[8,1]{0,1:T(1,128)}, f32[8,328,128]{2,1,0:T(8,128)S(1)}) %tuple.21, (s32[8,128]{1,0:T(8,128)S(1)}, f32[56,328,128]{2,1,0:T(8,128)}) %tuple.15), branch_computations={%region_0.4_spmd, %region_4.5_spmd} | conditional | flops 1824 | bytes 54413552 | solution.py:810
  70.7 4.0 %place.1 = f32[10368,128]{1,0:T(8,128)} custom-call(s32[8,128]{1,0:T(8,128)S(1)} %get-tuple-element.16.table, f32[56,328,128]{2,1,0:T(8,128)} %get-tuple-element.17.final), custom_call_target="tpu_custom_call" | custom-call | tf_op jit(solution)/shard_map/cond/branch_1_fun/place/pallas_call | solution.py:683
  74.7 0.0 copy-done
  74.7 0.7 copy.33
Async XLA Ops:
  70.4 4.3 %copy-start = (f32[3,128,256]{2,1,0:T(8,128)S(1)}, f32[3,128,256]{2,1,0:T(8,128)}, u32[]{:S(2)}) copy-start(f32[3,128,256]{2,1,0:T(8,128)} %get-tuple-element.32) | copy-start | bytes 1179652

commit v7 on v6

--- a/solution.py
+++ b/solution.py
@@ -415,7 +415,7 @@
         return hop(two, j, send2.at[pl.ds(low, n)], final.at[pl.ds(FINAL_RING + low, n)], y, 1 - z, 0)
 
     half = RING_SECOND // 3
-    pieces = tuple((j, h) for h in range(3) for j in range(3))
+    pieces = tuple((j, h) for h in range(3) for j in (2, 0, 1))
 
     def ring_second(i):
         j, h = pieces[i]

time: 75.8 us -> 75.6 us (level)
    pallas_call x1, Pallas kernels: 69.1 us -> 68.3 us  [local(): pl.pallas_call(lambda *refs: kernel(n_gore, n_band, *refs), out_shape=(ja...]
where the time goes in v7:
time: 75.6 us; the launch traced here: 75.1 us
  Pallas kernels  72.8 us (96%)
  between operations  1.34 us (2%)
    pallas_call x1, Pallas kernels, local(): pl.pallas_call(lambda *refs: kernel(n_gore, n_band, *refs), out_shape=(ja...  68.3 us
    pallas_call x1, Pallas kernels, place(): pl.pallas_call(place_kernel, out_shape=jax.ShapeDtypeStruct((3 * slots *...  4.44 us

profile of v7, /device:TPU:1, one launch (start us, length us, event | category | flops | bytes accessed | tf_op | source)
XLA Modules:
  0.0 75.1 jit_solution(12958292486319346137)
XLA Ops:
  0.6 68.3 %cells.1 = (f32[3,128,256]{2,1,0:T(8,128)}, s32[1]{0:T(128)}, s32[8,128]{1,0:T(8,128)S(1)}, f32[56,328,128]{2,1,0:T(8,128)}, f32[8,328,128]{2,1,0:T(8,128)S(1)}) custom-call(s32[8]{0:T(128)} %refs_0_.1, s32[8]{0:T(128)} %bitcast.24, f32[3,128,256]{2,1,0:T(8,128)} %refs_2_.1, f32[128,256]{1,0:T(8,128)} %refs_3_.1, f32[128,256]{1,0:T(8,128)} %refs_4_.1, ...), custom_call_target="tpu_custom_call" | custom-call | tf_op jit(solution)/shard_map/cells/pallas_call | solution.py:726
  69.6 0.0 copy-start
  69.7 4.7 %conditional.1 = (f32[3,32,13824]{2,1,0:T(8,128)}) conditional(s32[]{:T(128)} %bitcast.11, (s32[8]{0:T(128)}, s32[8,1]{0,1:T(1,128)}, f32[8,328,128]{2,1,0:T(8,128)S(1)}) %tuple.21, (s32[8,128]{1,0:T(8,128)S(1)}, f32[56,328,128]{2,1,0:T(8,128)}) %tuple.15), branch_computations={%region_0.4_spmd, %region_4.5_spmd} | conditional | flops 1824 | bytes 54413552 | solution.py:810
  69.9 4.4 %place.1 = f32[10368,128]{1,0:T(8,128)} custom-call(s32[8,128]{1,0:T(8,128)S(1)} %get-tuple-element.16.table, f32[56,328,128]{2,1,0:T(8,128)} %get-tuple-element.17.final), custom_call_target="tpu_custom_call" | custom-call | tf_op jit(solution)/shard_map/cond/branch_1_fun/place/pallas_call | solution.py:683
  74.3 0.0 copy-done
  74.3 0.7 copy.33
Async XLA Ops:
  69.6 4.7 %copy-start = (f32[3,128,256]{2,1,0:T(8,128)S(1)}, f32[3,128,256]{2,1,0:T(8,128)}, u32[]{:S(2)}) copy-start(f32[3,128,256]{2,1,0:T(8,128)} %get-tuple-element.32) | copy-start | bytes 1179652
